TPU v7x, 32 devices: a whole 2x2x4 slice. The times are simulated.
32 devices in a mesh: dp: 4 (over x, core), expert: 8 (over z, y).
Axes of the slice: x: 2, y: 2, z: 4, core: 2. Of those that a mesh axis runs over, the one named last changes fastest.
Arguments:
- tokens: bfloat16 [128, 2880], P(('dp', 'expert')), may hold values from -6 to 6
- cotangent: bfloat16 [128, 2880], P(('dp', 'expert')), may hold values from -6 to 6
- expert_ids: int32 [128, 4], P(('dp', 'expert')), may hold values from 0 to 7, all different within a row; in each aligned block of 4 rows (0 to 3, 4 to 7, ...) at most 2 rows name the same one
- route_weights: bfloat16 [128, 4], P(('dp', 'expert')), may hold values from 0.049804688 to 0.59765625
- gate_weight: bfloat16 [2880, 12288], P('dp', 'expert'), may hold values from -0.109375 to 0.109375
- up_weight: bfloat16 [2880, 12288], P('dp', 'expert'), may hold values from -0.109375 to 0.109375
- down_weight: bfloat16 [2880, 12288], P('dp', 'expert'), may hold values from -0.15625 to 0.15625
Outputs:
- d_tokens: bfloat16 [128, 2880], P(('dp', 'expert'))
- d_route: float32 [128, 4], P(('dp', 'expert'))
- grad_gate: bfloat16 [2880, 12288], P('dp', 'expert')
- grad_up: bfloat16 [2880, 12288], P('dp', 'expert')
- grad_down: bfloat16 [2880, 12288], P('dp', 'expert')
Inputs may be any that keep to these rules, and one draw needn't show every extreme that they name: `expert_ids`: among the 4 tokens of one device, every expert is named by exactly 2 of them; a token names 4 different experts.
All inputs are finite; a program needn't handle non-finite values.
Results may differ from a plain program's by a relative error of at most 0.009.
Values may be sent and summed in bfloat16 or wider, within the bound.
No kernel may reach another device: no remote copies, remote signals or barrier semaphores. Data moves between devices by JAX's collectives and lax.ppermute only.
A program may use at most 192 MiB of HBM per device.

v0:
```python
import jax
import jax.numpy as jnp
from jax import lax
from jax.sharding import PartitionSpec as P

EXPERTS_F = 8
TOPK = 4


SLOPE = 1.702


def contract_rows(left, right):
    return lax.dot_general(
        left, right, (((0,), (0,)), ((), ())), preferred_element_type=jnp.float32
    )


def contract_cols(left, right):
    return lax.dot_general(
        left, right, (((1,), (1,)), ((), ())), preferred_element_type=jnp.float32
    )


def local(tokens, cotangent, expert_ids, route_weights, gate_weight, up_weight, down_weight):
    members = lax.axis_size("expert")
    per_expert = members // EXPERTS_F
    token_count = tokens.shape[0]
    model_width = tokens.shape[1]
    hidden_units = gate_weight.shape[1]
    slots = token_count * TOPK // EXPERTS_F
    expert_iota = lax.iota(jnp.int32, EXPERTS_F)
    hits = expert_ids[:, :, None] == expert_iota[None, None, :]
    picked = jnp.any(hits, axis=1)
    weight_each = jnp.sum(
        jnp.where(hits, route_weights[:, :, None].astype(jnp.float32), 0.0), axis=1
    )
    ranking = jnp.cumsum(picked.astype(jnp.int32), axis=0) - 1
    slot_iota = lax.iota(jnp.int32, slots)
    selector = picked.T[:, None, :] & (ranking.T[:, None, :] == slot_iota[None, :, None])
    select_float = selector.astype(jnp.float32)
    select_low = selector.astype(jnp.bfloat16)
    bucket_tokens = jnp.einsum(
        "ect,td->ecd", select_low, tokens, preferred_element_type=jnp.float32
    ).astype(jnp.bfloat16)
    bucket_grads = jnp.einsum(
        "ect,td->ecd", select_low, cotangent, preferred_element_type=jnp.float32
    ).astype(jnp.bfloat16)
    bucket_factor = jnp.sum(select_float * weight_each.T[:, None, :], axis=2).astype(jnp.bfloat16)
    send_tokens = jnp.repeat(bucket_tokens, per_expert, axis=0)
    send_grads = jnp.repeat(bucket_grads, per_expert, axis=0)
    send_factor = jnp.repeat(bucket_factor, per_expert, axis=0)
    got_tokens, got_grads, got_factors = (
        lax.all_to_all(send_tokens, "expert", split_axis=0, concat_axis=0, tiled=True),
        lax.all_to_all(send_grads, "expert", split_axis=0, concat_axis=0, tiled=True),
        lax.all_to_all(send_factor, "expert", split_axis=0, concat_axis=0, tiled=True),
    )
    inputs = got_tokens.reshape(-1, model_width)
    upstream = got_grads.reshape(-1, model_width)
    factor = got_factors.reshape(-1).astype(jnp.float32)[:, None]
    joined = jnp.concatenate([gate_weight, up_weight], axis=1)
    joined_full, down_full = (
        lax.all_gather(joined, "dp", axis=0, tiled=True),
        lax.all_gather(down_weight, "dp", axis=0, tiled=True),
    )
    projected = jnp.dot(inputs, joined_full, preferred_element_type=jnp.float32)
    pulled = jnp.dot(upstream, down_full, preferred_element_type=jnp.float32)
    pre_gate = projected[:, :hidden_units]
    pre_up = projected[:, hidden_units:]
    sigma = jax.nn.sigmoid(SLOPE * pre_gate)
    active = pre_gate * sigma
    hidden = (pre_up + 1.0) * active
    partial_dots = jnp.sum(hidden * pulled, axis=1).astype(jnp.bfloat16)
    d_gate = (
        factor * pulled * (pre_up + 1.0) * sigma * (1.0 + SLOPE * pre_gate * (1.0 - sigma))
    ).astype(jnp.bfloat16)
    d_up = (factor * pulled * active).astype(jnp.bfloat16)
    d_joined = jnp.concatenate([d_gate, d_up], axis=1)
    d_inputs = contract_cols(d_joined, joined_full)
    back_inputs, back_dots = (
        lax.all_to_all(
            d_inputs.astype(jnp.bfloat16).reshape(members, slots, model_width),
            "expert",
            split_axis=0,
            concat_axis=0,
            tiled=True,
        ),
        lax.all_to_all(
            partial_dots.reshape(members, slots), "expert", split_axis=0, concat_axis=0, tiled=True
        ),
    )
    select_dev = jnp.repeat(select_low, per_expert, axis=0).reshape(members * slots, token_count)
    d_tokens = contract_rows(select_dev, back_inputs.reshape(members * slots, model_width)).astype(
        jnp.bfloat16
    )
    expert_dots = jnp.sum(
        back_dots.astype(jnp.float32).reshape(EXPERTS_F, per_expert, slots), axis=1
    )
    token_dots = jnp.sum(select_float * expert_dots[:, :, None], axis=1)
    d_route = jnp.sum(jnp.where(hits, token_dots.T[:, None, :], 0.0), axis=2)
    hidden_low = hidden.astype(jnp.bfloat16)
    scaled = (factor * upstream.astype(jnp.float32)).astype(jnp.bfloat16)
    summed = lax.psum_scatter(
        jnp.concatenate(
            [contract_rows(inputs, d_joined), contract_rows(scaled, hidden_low)], axis=1
        ).astype(jnp.bfloat16),
        "dp",
        scatter_dimension=0,
        tiled=True,
    ).astype(jnp.float32)
    grad_gate = summed[:, :hidden_units].astype(jnp.bfloat16)
    grad_up = summed[:, hidden_units : 2 * hidden_units].astype(jnp.bfloat16)
    grad_down = summed[:, 2 * hidden_units :].astype(jnp.bfloat16)
    return (d_tokens, d_route, grad_gate, grad_up, grad_down)


def solution(mesh):
    in_specs = (
        P(("dp", "expert"), None),
        P(("dp", "expert"), None),
        P(("dp", "expert"), None),
        P(("dp", "expert"), None),
        P("dp", "expert"),
        P("dp", "expert"),
        P("dp", "expert"),
    )
    out_specs = (
        P(("dp", "expert"), None),
        P(("dp", "expert"), None),
        P("dp", "expert"),
        P("dp", "expert"),
        P("dp", "expert"),
    )
    return jax.shard_map(local, mesh=mesh, in_specs=in_specs, out_specs=out_specs, check_vma=False)
```

profile of v0, /device:TPU:0, one launch (start us, length us, event | category | flops | bytes accessed | tf_op | source)
XLA Modules:
  0.0 450.0 jit_solution(16410950239695207048)
XLA Ops:
  7.2 0.0 copy-start
  7.2 0.0 copy-start.3
  7.2 0.0 copy-start.2
  7.2 0.0 all-gather.5.cloned.1.call-start
  7.2 4.9 %pad_maximum_fusion.1 = bf16[720,3072]{1,0:T(8,128)(2,1)} fusion(bf16[720,1536]{1,0:T(8,128)(2,1)} %param.12, bf16[720,1536]{1,0:T(8,128)(2,1)} %param.11), kind=kLoop, calls=%fused_computation.3 | loop fusion | flops 8847360 | bytes 8847360 | tf_op jit(solution)/shard_map/concatenate | solution.py:61
  12.1 0.0 all-gather.5.cloned.1.call-update
  12.1 0.0 all-gather.3.cloned.1.call-start
  12.2 0.7 all-gather.3.cloned.1.call-update
  12.9 0.0 copy-done.3
  12.9 0.1 fusion.7
  13.1 0.0 copy-done
  13.1 0.2 convolution_convert_fusion.3
  13.3 0.7 copy.34
  14.0 7.3 %all-to-all-start.2 = ((bf16[8,2,2880]{2,1,0:T(2,128)(2,1)}), bf16[8,2,2880]{2,1,0:T(2,128)(2,1)S(1)}, u32[]{:S(2)}, u32[]{:S(2)}) async-start(bf16[8,2,2880]{2,1,0:T(2,128)(2,1)} %copy.34), calls=%async_computation.2 | async-start | bytes 188416 | tf_op jit(solution)/shard_map/all_to_all | solution.py:54
  21.3 0.0 copy-done.2
  21.3 0.2 convolution_convert_fusion.4
  21.5 0.7 copy.33
  22.2 6.2 %all-to-all-done.2 = bf16[8,2,2880]{2,1,0:T(2,128)(2,1)S(1)} async-done(((bf16[8,2,2880]{2,1,0:T(2,128)(2,1)}), bf16[8,2,2880]{2,1,0:T(2,128)(2,1)S(1)}, u32[]{:S(2)}, u32[]{:S(2)}) %all-to-all-start.2) | async-done | bytes 92192 | tf_op jit(solution)/shard_map/all_to_all | solution.py:54
  28.4 3.4 all-to-all-start.1
  31.8 0.1 reshape.66
  31.8 7.0 %all-to-all-done.1 = bf16[8,2,2880]{2,1,0:T(2,128)(2,1)S(1)} async-done(((bf16[8,2,2880]{2,1,0:T(2,128)(2,1)}), bf16[8,2,2880]{2,1,0:T(2,128)(2,1)S(1)}, u32[]{:S(2)}, u32[]{:S(2)}) %all-to-all-start.1) | async-done | bytes 92192 | tf_op jit(solution)/shard_map/all_to_all | solution.py:55
  38.8 0.1 reshape.65
  38.9 89.6 %all-gather.5.cloned.1.call-done = bf16[2880,3072]{1,0:T(8,128)(2,1)} async-done(((bf16[720,3072]{1,0:T(8,128)(2,1)}), bf16[2880,3072]{1,0:T(8,128)(2,1)}) %all-gather.5.cloned.1.call-update) | async-done | bytes 17694736 | tf_op jit(solution)/shard_map/all_gather | solution.py:63
  128.5 7.3 %fusion.13 = f32[16,3072]{1,0:T(8,128)S(1)} fusion(bf16[16,2880]{1,0:T(8,128)(2,1)S(1)} %reshape.66, bf16[2880,3072]{1,0:T(8,128)(2,1)} %all-gather.5.cloned.1.call-done), kind=kOutput, calls=%fused_computation.39 | convolution fusion | flops 283115520 | bytes 17983488 | tf_op jit(solution)/shard_map/dot_general | solution.py:66
  135.8 55.2 %all-gather.3.cloned.1.call-done = bf16[2880,1536]{1,0:T(8,128)(2,1)} async-done(((bf16[720,1536]{1,0:T(8,128)(2,1)}), bf16[2880,1536]{1,0:T(8,128)(2,1)}) %all-gather.3.cloned.1.call-update) | async-done | bytes 8847376 | tf_op jit(solution)/shard_map/all_gather | solution.py:64
  191.0 4.9 %multiply_reduce_fusion = (bf16[16]{0:T(256)(128)(2,1)S(1)}, f32[16,1536]{1,0:T(8,128)S(1)}) fusion(f32[16,3072]{1,0:T(8,128)S(1)} %fusion.13, bf16[16,2880]{1,0:T(8,128)(2,1)S(1)} %reshape.65, bf16[2880,1536]{1,0:T(8,128)(2,1)} %all-gather.3.cloned.1.call-done), kind=kOutput, calls=%fused_computation.12 | convolution fusion | flops 141778928 | bytes 9234464 | tf_op jit(solution)/shard_map/dot_general | solution.py:67
  195.9 0.7 convert_element_type.98
  196.5 5.5 %all-to-all-start.4 = ((bf16[8,1,2]{2,1,0:T(2,128)(2,1)}), bf16[8,1,2]{2,1,0:T(2,128)(2,1)S(1)}, u32[]{:S(2)}, u32[]{:S(2)}) async-start(bf16[8,1,2]{2,1,0:T(2,128)(2,1)} %convert_element_type.98), calls=%async_computation.4 | async-start | bytes 8192 | tf_op jit(solution)/shard_map/all_to_all | solution.py:88
  202.1 0.0 reduce-scatter.2.cloned.1.call-start
  202.1 6.3 %all-to-all-done.4 = bf16[8,1,2]{2,1,0:T(2,128)(2,1)S(1)} async-done(((bf16[8,1,2]{2,1,0:T(2,128)(2,1)}), bf16[8,1,2]{2,1,0:T(2,128)(2,1)S(1)}, u32[]{:S(2)}, u32[]{:S(2)}) %all-to-all-start.4) | async-done | bytes 64 | tf_op jit(solution)/shard_map/all_to_all | solution.py:88
  208.5 0.1 copy.37
  208.6 0.7 select_reduce_fusion
  209.3 0.1 copy.32
  209.4 8.8 %all_to_all.27 = bf16[8,1,2]{2,1,0:T(2,128)(2,1)S(1)} all-to-all(bf16[8,1,2]{2,1,0:T(2,128)(2,1)S(1)} %copy.32), channel_id=1, replica_groups=mesh['dp'=4,'expert'=8] {'expert'}, dimensions={0} | all-to-all | bytes 64 | tf_op jit(solution)/shard_map/all_to_all | solution.py:56
  218.3 0.1 reshape.68
  218.4 6.0 %convolution_convert_fusion.1 = bf16[2880,1536]{1,0:T(8,128)(2,1)} fusion(bf16[16,2880]{1,0:T(8,128)(2,1)S(1)} %reshape.65, f32[16]{0:T(128)S(1)} %reshape.68, f32[16,3072]{1,0:T(8,128)S(1)} %fusion.13), kind=kOutput, calls=%fused_computation.2 | convolution fusion | flops 146316288 | bytes 9136192 | tf_op jit(solution)/shard_map/dot_general | solution.py:14
  224.3 0.1 multiply_convert_fusion.2
  224.4 8.8 %convolution_convert_fusion = bf16[2880,3072]{1,0:T(8,128)(2,1)} fusion(bf16[16,2880]{1,0:T(8,128)(2,1)S(1)} %reshape.66, bf16[16,1536]{1,0:T(8,128)(2,1)S(1)} %get-tuple-element.11, bf16[16,1536]{1,0:T(8,128)(2,1)S(1)} %get-tuple-element.10), kind=kOutput, calls=%fused_computation.1 | convolution fusion | flops 292159488 | bytes 17885184 | tf_op jit(solution)/shard_map/dot_general | solution.py:14
  233.2 18.4 %pad_maximum_fusion = bf16[2880,4608]{1,0:T(8,128)(2,1)} fusion(bf16[2880,1536]{1,0:T(8,128)(2,1)} %convolution_convert_fusion.1, bf16[2880,3072]{1,0:T(8,128)(2,1)} %convolution_convert_fusion), kind=kLoop, calls=%fused_computation | loop fusion | flops 53084160 | bytes 53084160 | tf_op jit(solution)/shard_map/concatenate | solution.py:104
  251.7 0.0 reduce-scatter.2.cloned.1.call-update
  251.7 0.0 copy-start.1
  251.7 13.9 %convolution_convert_fusion.2 = bf16[16,2880]{1,0:T(8,128)(2,1)S(1)} fusion(bf16[2880,3072]{1,0:T(8,128)(2,1)} %all-gather.5.cloned.1.call-done, bf16[16,1536]{1,0:T(8,128)(2,1)S(1)} %get-tuple-element.11, bf16[16,1536]{1,0:T(8,128)(2,1)S(1)} %get-tuple-element.10), kind=kOutput, calls=%fused_computation.4 | convolution fusion | flops 283358208 | bytes 17885184 | tf_op jit(solution)/shard_map/dot_general | solution.py:20
  265.7 0.1 reshape.67
  265.7 9.5 %all_to_all.28 = bf16[8,2,2880]{2,1,0:T(2,128)(2,1)S(1)} all-to-all(bf16[8,2,2880]{2,1,0:T(2,128)(2,1)S(1)} %reshape.67), channel_id=1, replica_groups=mesh['dp'=4,'expert'=8] {'expert'}, dimensions={0} | all-to-all | bytes 184320 | tf_op jit(solution)/shard_map/all_to_all | solution.py:81
  275.2 0.8 fusion
  276.0 161.5 %reduce-scatter.2.cloned.1.call-done = bf16[720,4608]{1,0:T(8,128)(2,1)} async-done(((bf16[2880,4608]{1,0:T(8,128)(2,1)}), bf16[720,4608]{1,0:T(8,128)(2,1)}) %reduce-scatter.2.cloned.1.call-update) | async-done | bytes 6635536 | tf_op jit(solution)/shard_map/reduce_scatter | solution.py:103
  437.6 5.9 %fusion.12 = (bf16[720,1536]{1,0:T(8,128)(2,1)}, bf16[720,1536]{1,0:T(8,128)(2,1)}, bf16[720,1536]{1,0:T(8,128)(2,1)}) fusion(bf16[720,4608]{1,0:T(8,128)(2,1)} %reduce-scatter.2.cloned.1.call-done), kind=kLoop, calls=%fused_computation.38 | loop fusion | bytes 13271040 | tf_op jit(solution)/shard_map/slice | solution.py:113
  443.5 0.0 copy-done.1
  (11 shorter events, 0.1 us)
Async XLA Ops:
  7.2 5.9 %copy-start = (bf16[4,2880]{1,0:T(4,128)(2,1)S(1)}, bf16[4,2880]{1,0:T(4,128)(2,1)}, u32[]{:S(2)}) copy-start(bf16[4,2880]{1,0:T(4,128)(2,1)} %param.7) | copy-start | bytes 69124
  7.2 5.7 %copy-start.3 = (s32[4,4]{1,0:T(4,128)S(1)}, s32[4,4]{1,0:T(4,128)}, u32[]{:S(2)}) copy-start(s32[4,4]{1,0:T(4,128)} %param.9) | copy-start | bytes 196
  7.2 14.1 %copy-start.2 = (bf16[4,2880]{1,0:T(4,128)(2,1)S(1)}, bf16[4,2880]{1,0:T(4,128)(2,1)}, u32[]{:S(2)}) copy-start(bf16[4,2880]{1,0:T(4,128)(2,1)} %param.8) | copy-start | bytes 69124
  7.2 121.3 %all-gather.5.cloned.1.call-start = ((), (), s32[]{:S(2)}) async-start(), calls=%async_computation.7 | async-start | bytes 22118400 | tf_op jit(solution)/shard_map/all_gather | solution.py:63
  12.1 178.8 %all-gather.3.cloned.1.call-start = ((), (), s32[]{:S(2)}) async-start(), calls=%async_computation.6 | async-start | bytes 11059200 | tf_op jit(solution)/shard_map/all_gather | solution.py:64
  14.0 14.4 %all-to-all-start.2 = ((bf16[8,2,2880]{2,1,0:T(2,128)(2,1)}), bf16[8,2,2880]{2,1,0:T(2,128)(2,1)S(1)}, u32[]{:S(2)}, u32[]{:S(2)}) async-start(bf16[8,2,2880]{2,1,0:T(2,128)(2,1)} %copy.34), calls=%async_computation.2 | async-start | bytes 188416 | tf_op jit(solution)/shard_map/all_to_all | solution.py:54
  28.4 10.4 %all-to-all-start.1 = ((bf16[8,2,2880]{2,1,0:T(2,128)(2,1)}), bf16[8,2,2880]{2,1,0:T(2,128)(2,1)S(1)}, u32[]{:S(2)}, u32[]{:S(2)}) async-start(bf16[8,2,2880]{2,1,0:T(2,128)(2,1)} %copy.33), calls=%async_computation.1 | async-start | bytes 188416 | tf_op jit(solution)/shard_map/all_to_all | solution.py:55
  135.8 66.3 %copy-start.4 = (bf16[4,4]{1,0:T(4,128)(2,1)S(1)}, bf16[4,4]{1,0:T(4,128)(2,1)}, u32[]{:S(2)}) copy-start(bf16[4,4]{1,0:T(4,128)(2,1)} %param.10) | copy-start | bytes 100
  196.5 11.9 %all-to-all-start.4 = ((bf16[8,1,2]{2,1,0:T(2,128)(2,1)}), bf16[8,1,2]{2,1,0:T(2,128)(2,1)S(1)}, u32[]{:S(2)}, u32[]{:S(2)}) async-start(bf16[8,1,2]{2,1,0:T(2,128)(2,1)} %convert_element_type.98), calls=%async_computation.4 | async-start | bytes 8192 | tf_op jit(solution)/shard_map/all_to_all | solution.py:88
  202.1 235.5 %reduce-scatter.2.cloned.1.call-start = ((), (), s32[]{:S(2)}) async-start(), calls=%async_computation.8 | async-start | bytes 33177600 | tf_op jit(solution)/shard_map/reduce_scatter | solution.py:103
  251.7 191.8 %copy-start.1 = (bf16[4,2880]{1,0:T(4,128)(2,1)S(1)}, bf16[4,2880]{1,0:T(4,128)(2,1)}, u32[]{:S(2)}) copy-start(bf16[4,2880]{1,0:T(4,128)(2,1)} %param.7) | copy-start | bytes 69124
Sparse Core Ops, SparseCore 0:
  12.3 116.1 all-gather.4
  130.0 60.8 all-gather.2
  251.8 185.7 reduce-scatter.1
where the time goes:
time: 451 us; the launch traced here: 450 us
  waiting for transfers between devices  327 us (73%)
  matrix products  42.2 us (9%)
  other arithmetic  24.3 us (5%)
  blocking collectives  18.3 us (4%)
  starting transfers between devices  16.3 us (4%)
  between operations  13.9 us (3%)
  local copies, waits for them, and re-layouts  8.58 us (2%)
    reduce_scatter x1, waiting for transfers between devices, local(): lax.psum_scatter(jnp.concatenate([contract_rows(inputs, d_joined), contra...  162 us
    all_gather x1, waiting for transfers between devices, local(): lax.all_gather(joined, 'dp', axis=0, tiled=True)  89.6 us
    all_gather x1, waiting for transfers between devices, local(): lax.all_gather(down_weight, 'dp', axis=0, tiled=True)  55.2 us
    concatenate x1, other arithmetic, local(): jnp.concatenate([contract_rows(inputs, d_joined), contract_rows(scaled, h...  18.4 us
    dot_general x3, matrix products, contract_rows(): lax.dot_general(left, right, (((0,), (0,)), ((), ())), preferred_element_...  15.6 us
    dot_general x1, matrix products, contract_cols(): lax.dot_general(left, right, (((1,), (1,)), ((), ())), preferred_element_...  13.9 us
    all_to_all x1, blocking collectives, local(): lax.all_to_all(d_inputs.astype(jnp.bfloat16).reshape(members, slots, mode...  9.48 us
  transfers between devices with their start and end apart: 6, of which 6 were waited for; matrix products, arithmetic and copies ran while one was open for 5% of the time, Pallas kernels for 0%

commit v1 on v0

v1 whole, which is shorter than its diff:
```python
import jax
import jax.numpy as jnp
from jax import lax
from jax.sharding import PartitionSpec as P

EXPERTS_F = 8
TOPK = 4
CORES = 2
LANES = 128


SLOPE = 1.702


def contract_rows(left, right):
    return lax.dot_general(
        left, right, (((0,), (0,)), ((), ())), preferred_element_type=jnp.float32
    )


def contract_cols(left, right):
    return lax.dot_general(
        left, right, (((1,), (1,)), ((), ())), preferred_element_type=jnp.float32
    )


def round_up(value, unit):
    return (value + unit - 1) // unit * unit


def local(tokens, cotangent, expert_ids, route_weights, gate_weight, up_weight, down_weight):
    n_dp = lax.axis_size("dp")
    members = lax.axis_size("expert")
    per_expert = members // EXPERTS_F
    sources = n_dp * members
    token_count, model_width = tokens.shape
    rows, hidden_units = gate_weight.shape
    half = hidden_units // CORES
    slots = token_count * TOPK // EXPERTS_F
    bf16 = jnp.bfloat16
    wide = round_up(rows // 2 + 1, LANES)

    expert_iota = lax.iota(jnp.int32, EXPERTS_F)
    hits = expert_ids[:, :, None] == expert_iota[None, None, :]
    picked = jnp.any(hits, axis=1)
    weight_each = jnp.sum(
        jnp.where(hits, route_weights[:, :, None].astype(jnp.float32), 0.0), axis=1
    )
    ranking = jnp.cumsum(picked.astype(jnp.int32), axis=0) - 1
    slot_iota = lax.iota(jnp.int32, slots)
    selector = picked.T[:, None, :] & (ranking.T[:, None, :] == slot_iota[None, :, None])
    select_float = selector.astype(jnp.float32)
    select_low = selector.astype(bf16)

    def bucket(x):
        b = jnp.einsum("ect,td->ecd", select_low, x, preferred_element_type=jnp.float32).astype(bf16)
        return b.reshape(EXPERTS_F, slots, n_dp, rows)

    bucket_tokens = bucket(tokens)
    bucket_grads = bucket(cotangent)
    bucket_factor = jnp.sum(select_float * weight_each.T[:, None, :], axis=2).astype(bf16)
    spare = 2 * wide - rows
    factor_pad = jnp.zeros((EXPERTS_F, slots, n_dp, spare), bf16).at[..., 0].set(bucket_factor[:, :, None])
    packed = jnp.stack(
        [jnp.concatenate([bucket_tokens, factor_pad], -1), jnp.concatenate([bucket_grads, factor_pad], -1)], axis=0
    ).reshape(2, EXPERTS_F, slots, n_dp, 2, wide)
    packed = packed.transpose(3, 1, 0, 4, 2, 5)
    packed = jnp.repeat(packed, per_expert, axis=1).reshape(sources, 4 * slots, wide)
    got = lax.all_to_all(packed, ("dp", "expert"), split_axis=0, concat_axis=0, tiled=True)
    got = got.reshape(sources, 2, 2, slots, wide).transpose(1, 0, 3, 2, 4).reshape(2, sources * slots, 2 * wide)
    inputs = got[0, :, :rows]
    upstream = got[1, :, :rows]
    factor = got[0, :, rows : rows + 1].astype(jnp.float32)
    count = sources * slots

    me = lax.axis_index("dp")
    core = lax.rem(me, CORES)
    part = jnp.stack(
        [
            jnp.dot(inputs, gate_weight, preferred_element_type=jnp.float32),
            jnp.dot(inputs, up_weight, preferred_element_type=jnp.float32),
            jnp.dot(upstream, down_weight, preferred_element_type=jnp.float32),
        ],
        axis=1,
    )
    keep = lax.dynamic_slice_in_dim(part, core * half, half, 2)
    send = lax.dynamic_slice_in_dim(part, (1 - core) * half, half, 2).astype(bf16)
    swap = [(i, i ^ 1) for i in range(n_dp)]
    pair = keep + lax.ppermute(send, "dp", swap).astype(jnp.float32)
    chips = n_dp // CORES
    pair_low = pair.astype(bf16)
    total = pair
    for shift in range(1, chips):
        perm = [(i, (i + shift * CORES) % n_dp) for i in range(n_dp)]
        total = total + lax.ppermute(pair_low, "dp", perm).astype(jnp.float32)
    pre_gate, pre_up, pulled = total[:, 0], total[:, 1], total[:, 2]
    sigma = jax.nn.sigmoid(SLOPE * pre_gate)
    active = pre_gate * sigma
    hidden = (pre_up + 1.0) * active
    dots = jnp.sum(hidden * pulled, axis=1, keepdims=True)
    d_gate = factor * pulled * (pre_up + 1.0) * sigma * (1.0 + SLOPE * pre_gate * (1.0 - sigma))
    d_up = factor * pulled * active
    own = jnp.stack([d_gate, d_up, hidden], axis=1).astype(bf16)
    other = lax.ppermute(own, "dp", swap)
    full = jnp.where(core == 0, jnp.concatenate([own, other], 2), jnp.concatenate([other, own], 2))
    d_gate, d_up, hidden_low = full[:, 0], full[:, 1], full[:, 2]

    d_inputs = contract_cols(d_gate, gate_weight) + contract_cols(d_up, up_weight)
    dots_high = dots.astype(bf16)
    dots_rest = (dots - dots_high.astype(jnp.float32)).astype(bf16)
    back_wide = round_up(rows + 2, LANES)
    back = jnp.concatenate(
        [d_inputs.astype(bf16), dots_high, dots_rest, jnp.zeros((count, back_wide - rows - 2), bf16)], axis=1
    ).reshape(sources, slots, back_wide)
    back = lax.all_to_all(back, ("dp", "expert"), split_axis=0, concat_axis=0, tiled=True)
    back = back.reshape(n_dp, members * slots, back_wide)

    scaled = (factor * upstream.astype(jnp.float32)).astype(bf16)
    grad_gate = contract_rows(inputs, d_gate).astype(bf16)
    grad_up = contract_rows(inputs, d_up).astype(bf16)
    grad_down = contract_rows(scaled, hidden_low).astype(bf16)

    select_dev = jnp.repeat(select_low, per_expert, axis=0).reshape(members * slots, token_count)
    d_tokens = jnp.einsum("st,nsd->tnd", select_dev, back[:, :, :rows], preferred_element_type=jnp.float32)
    d_tokens = d_tokens.astype(bf16).reshape(token_count, model_width)
    back_dots = back[:CORES, :, rows : rows + 2].astype(jnp.float32)
    expert_dots = jnp.sum(back_dots, axis=(0, 2)).reshape(EXPERTS_F, per_expert, slots).sum(axis=1)
    token_dots = jnp.sum(select_float * expert_dots[:, :, None], axis=1)
    d_route = jnp.sum(jnp.where(hits, token_dots.T[:, None, :], 0.0), axis=2)
    return (d_tokens, d_route, grad_gate, grad_up, grad_down)


def solution(mesh):
    in_specs = (
        P(("dp", "expert"), None),
        P(("dp", "expert"), None),
        P(("dp", "expert"), None),
        P(("dp", "expert"), None),
        P("dp", "expert"),
        P("dp", "expert"),
        P("dp", "expert"),
    )
    out_specs = (
        P(("dp", "expert"), None),
        P(("dp", "expert"), None),
        P("dp", "expert"),
        P("dp", "expert"),
        P("dp", "expert"),
    )
    return jax.shard_map(local, mesh=mesh, in_specs=in_specs, out_specs=out_specs, check_vma=False)
```

time: 451 us -> 65.1 us (0.14)
  waiting for transfers between devices: 327 us -> 23.6 us
  matrix products: 42.2 us -> 13.3 us
  blocking collectives: 18.3 us -> 0 us
  other arithmetic: 24.3 us -> 10.1 us
  between operations: 13.9 us -> 0.95 us
    reduce_scatter x1 -> x0, waiting for transfers between devices: 162 us -> none  [local(): lax.psum_scatter(jnp.concatenate([contract_rows(inputs, d_joined), contra...]
    all_gather x2 -> x0, waiting for transfers between devices: 145 us -> none  [the longest x1 89.6 us: local(): lax.all_gather(joined, 'dp', axis=0, tiled=True)]
    concatenate x2, other arithmetic: 23.3 us -> 0.88 us  [the longest x1 0.79 us: local(): jnp.concatenate([d_inputs.astype(bf16), dots_high, dots_rest, jnp.zeros((...]
    all_to_all x2 -> x0, blocking collectives: 18.3 us -> none  [the longest x1 9.48 us: local(): lax.all_to_all(d_inputs.astype(jnp.bfloat16).reshape(members, slots, mode...]
    dot_general x1 -> x2, matrix products: 13.9 us -> 1.56 us  [contract_cols(): lax.dot_general(left, right, (((1,), (1,)), ((), ())), preferred_element_...]
    ppermute x0 -> x3, waiting for transfers between devices: none -> 9.67 us  [the longest x1 6.83 us: local(): total = total + lax.ppermute(pair_low, 'dp', perm).astype(jnp.float32)]
    dot_general x3, matrix products: 15.6 us -> 6.42 us  [contract_rows(): lax.dot_general(left, right, (((0,), (0,)), ((), ())), preferred_element_...]
    dot_general x4 -> x6, matrix products: 12.6 us -> 5.28 us  [the longest x1 2.27 us: local(): jnp.dot(inputs, up_weight, preferred_element_type=jnp.float32)]
  transfers between devices with their start and end apart: 6 -> 5, of which waited for: 6 -> 5; matrix products, arithmetic and copies ran while one was open for 5% -> 6% of each run, Pallas kernels for 0% -> 0%
where the time goes in v1:
time: 65.1 us; the launch traced here: 64.5 us
  waiting for transfers between devices  23.6 us (36%)
  matrix products  13.3 us (20%)
  starting transfers between devices  11.9 us (18%)
  other arithmetic  10.1 us (16%)
  local copies, waits for them, and re-layouts  4.71 us (7%)
  between operations  0.95 us (1%)
    all_to_all x1, waiting for transfers between devices, local(): lax.all_to_all(packed, ('dp', 'expert'), split_axis=0, concat_axis=0, til...  8.53 us
    all_to_all x1, starting transfers between devices, local(): lax.all_to_all(packed, ('dp', 'expert'), split_axis=0, concat_axis=0, til...  7.3 us
    ppermute x1, waiting for transfers between devices, local(): total = total + lax.ppermute(pair_low, 'dp', perm).astype(jnp.float32)  6.83 us
    dot_general x3, matrix products, contract_rows(): lax.dot_general(left, right, (((0,), (0,)), ((), ())), preferred_element_...  6.42 us
    all_to_all x1, waiting for transfers between devices, local(): lax.all_to_all(back, ('dp', 'expert'), split_axis=0, concat_axis=0, tiled...  5.44 us
    all_to_all x1, starting transfers between devices, local(): lax.all_to_all(back, ('dp', 'expert'), split_axis=0, concat_axis=0, tiled...  3.03 us
    dot_general x1, matrix products, local(): jnp.dot(inputs, up_weight, preferred_element_type=jnp.float32)  2.27 us
    dot_general x2, matrix products, bucket(): jnp.einsum('ect,td->ecd', select_low, x, preferred_element_type=jnp.float32)  1.9 us
  transfers between devices with their start and end apart: 5, of which 5 were waited for; matrix products, arithmetic and copies ran while one was open for 6% of the time, Pallas kernels for 0%

profile of v1, /device:TPU:0, one launch (start us, length us, event | category | flops | bytes accessed | tf_op | source)
XLA Modules:
  0.0 64.5 jit_solution(281207847900334762)
XLA Ops:
  0.6 0.9 %fusion.22 = pred[4,8]{1,0:T(4,128)(4,1)S(1)} fusion(s32[4,4]{1,0:T(4,128)} %param.11), kind=kLoop, calls=%fused_computation.62 | loop fusion | flops 224 | bytes 96 | tf_op jit(solution)/shard_map/reduce_or | solution.py:45
  1.6 0.1 copy.70
  1.8 0.7 %convert_element_type.117 = f32[4,4]{1,0:T(4,128)S(1)} convert(bf16[4,4]{1,0:T(4,128)(2,1)} %param.12) | non-fusion elementwise | flops 16 | bytes 96 | tf_op jit(solution)/shard_map/convert_element_type | solution.py:47
  2.5 0.8 %select_reduce_fusion.3 = f32[4,8]{1,0:T(4,128)S(1)} fusion(f32[4,4]{1,0:T(4,128)S(1)} %convert_element_type.117, s32[4,4]{1,0:T(4,128)} %param.11), kind=kLoop, calls=%fused_computation.60 | loop fusion | flops 352 | bytes 256 | tf_op jit(solution)/shard_map/reduce_sum | solution.py:46
  3.3 0.1 select_reduce_fusion.2
  3.4 0.1 copy.76
  3.5 0.1 copy.74
  3.6 0.9 %convolution_convert_fusion = bf16[8,2,2880]{2,0,1:T(8,128)(2,1)S(1)} fusion(pred[8,2,4]{0,2,1:T(4,128)(4,1)S(1)} %copy.74, bf16[4,2880]{1,0:T(4,128)(2,1)} %param.10), kind=kOutput, calls=%fused_computation | convolution fusion | flops 414720 | bytes 115264 | tf_op jit(solution)/shard_map/ect,td->ecd/dot_general | solution.py:56
  4.6 0.2 reshape.157
  4.8 0.9 %convolution_convert_fusion.1 = bf16[8,2,2880]{2,0,1:T(8,128)(2,1)S(1)} fusion(pred[8,2,4]{0,2,1:T(4,128)(4,1)S(1)} %copy.74, bf16[4,2880]{1,0:T(4,128)(2,1)} %param.9), kind=kOutput, calls=%fused_computation.1 | convolution fusion | flops 414720 | bytes 115264 | tf_op jit(solution)/shard_map/ect,td->ecd/dot_general | solution.py:56
  5.7 0.2 reshape.156
  6.2 0.3 maximum_bitcast_fusion
  6.5 0.7 %copy.81 = bf16[32,8,384]{2,1,0:T(8,128)(2,1)} copy(bf16[32,8,384]{2,0,1:T(8,128)(2,1)S(1)} %bitcast.92) | data formatting | bytes 393216 | tf_op jit(solution)/shard_map/reshape;reshape;broadcast_in_dim | solution.py:68
  7.2 7.3 %all-to-all-start = ((bf16[32,8,384]{2,1,0:T(8,128)(2,1)}), bf16[32,8,384]{2,1,0:T(8,128)(2,1)S(1)}, u32[]{:S(2)}, u32[]{:S(2)}) async-start(bf16[32,8,384]{2,1,0:T(8,128)(2,1)} %copy.81), calls=%async_computation | async-start | bytes 393216 | tf_op jit(solution)/shard_map/all_to_all | solution.py:69
  14.5 8.5 %all-to-all-done = bf16[32,8,384]{2,1,0:T(8,128)(2,1)S(1)} async-done(((bf16[32,8,384]{2,1,0:T(8,128)(2,1)}), bf16[32,8,384]{2,1,0:T(8,128)(2,1)S(1)}, u32[]{:S(2)}, u32[]{:S(2)}) %all-to-all-start) | async-done | bytes 196640 | tf_op jit(solution)/shard_map/all_to_all | solution.py:69
  23.1 0.2 copy.83
  23.3 0.1 reshape.159
  23.5 2.3 %convolution_bitcast_fusion.1 = f32[64,1,1536]{2,0,1:T(8,128)S(1)} fusion(bf16[720,1536]{1,0:T(8,128)(2,1)} %param.14, bf16[2,64,768]{2,1,0:T(8,128)(2,1)S(1)} %reshape.159), kind=kOutput, calls=%fused_computation.6 | convolution fusion | flops 141557760 | bytes 2703360 | tf_op jit(solution)/shard_map/dot_general | solution.py:81
  25.8 0.5 convolution_bitcast_fusion
  26.3 0.5 convolution_bitcast_fusion.2
  26.9 0.8 %dynamic-slice_convert_fusion = bf16[64,3,768]{2,0,1:T(8,128)(2,1)} fusion(f32[64,3,1536]{2,0,1:T(8,128)S(1)} %pad_maximum_fusion, s32[]{:T(128)S(6)} %select_n.25), kind=kLoop, calls=%fused_computation.15 | loop fusion | bytes 589828 | tf_op jit(solution)/shard_map/convert_element_type | solution.py:87
  27.7 0.2 collective-permute-start
  27.9 1.8 %collective-permute-done = bf16[64,3,768]{2,0,1:T(8,128)(2,1)} collective-permute-done((bf16[64,3,768]{2,0,1:T(8,128)(2,1)}, bf16[64,3,768]{2,0,1:T(8,128)(2,1)}, u32[]{:S(2)}, u32[]{:S(2)}) %collective-permute-start) | collective-permute-done | bytes 294944 | tf_op jit(solution)/shard_map/ppermute | solution.py:89
  29.6 1.7 %fusion.1 = bf16[64,3,768]{2,0,1:T(8,128)(2,1)} fusion(bf16[64,3,768]{2,0,1:T(8,128)(2,1)} %collective-permute-done, f32[64,3,1536]{2,0,1:T(8,128)S(1)} %pad_maximum_fusion, s32[]{:T(128)S(6)} %select_n.24), kind=kLoop, calls=%fused_computation.16 | loop fusion | flops 442368 | bytes 1179652 | tf_op jit(solution)/shard_map/convert_element_type | solution.py:91
  31.3 1.3 %collective-permute-start.1 = (bf16[64,3,768]{2,0,1:T(8,128)(2,1)}, bf16[64,3,768]{2,0,1:T(8,128)(2,1)}, u32[]{:S(2)}, u32[]{:S(2)}) collective-permute-start(bf16[64,3,768]{2,0,1:T(8,128)(2,1)} %fusion.1), channel_id=1, source_target_pairs={{0,16},{8,24},{16,0},{24,8},{1,17},{9,25},{17,1},{25,9},{2,18},{10... | collective-permute-start | bytes 884744 | tf_op jit(solution)/shard_map/ppermute | solution.py:95
  32.7 0.1 copy.90
  33.0 0.9 %convert_reduce_fusion = f32[64]{0:T(128)S(1)} fusion(bf16[2,64,768]{2,1,0:T(8,128)(2,1)} %copy-done.2), kind=kLoop, calls=%fused_computation.52 | loop fusion | flops 64 | bytes 384 | tf_op jit(solution)/shard_map/convert_element_type | solution.py:73
  33.9 6.8 %collective-permute-done.1 = bf16[64,3,768]{2,0,1:T(8,128)(2,1)} collective-permute-done((bf16[64,3,768]{2,0,1:T(8,128)(2,1)}, bf16[64,3,768]{2,0,1:T(8,128)(2,1)}, u32[]{:S(2)}, u32[]{:S(2)}) %collective-permute-start.1) | collective-permute-done | bytes 294944 | tf_op jit(solution)/shard_map/ppermute | solution.py:95
  40.8 1.1 %convert_add_fusion = f32[64,3,768]{2,0,1:T(8,128)S(1)} fusion(bf16[64,3,768]{2,0,1:T(8,128)(2,1)} %collective-permute-done.1, bf16[64,3,768]{2,0,1:T(8,128)(2,1)} %collective-permute-done, f32[64,3,1536]{2,0,1:T(8,128)S(1)} %pad_maximum_fusion, s32[]{:T(128)S(6)} %select_n.24), kind=kLoop, calls=%fused_computation.13 | loop fusion | flops 589824 | bytes 1769476 | tf_op jit(solution)/shard_map/add | solution.py:95
  41.9 0.2 multiply_convert_fusion.3
  42.2 0.2 fusion.2
  42.4 0.1 reduce_sum.63
  42.6 0.1 copy.87
  42.7 0.1 copy.86
  42.8 1.1 %collective-permute-done.2 = bf16[64,3,768]{2,0,1:T(8,128)(2,1)} collective-permute-done((bf16[64,3,768]{2,0,1:T(8,128)(2,1)S(1)}, bf16[64,3,768]{2,0,1:T(8,128)(2,1)}, u32[]{:S(2)}, u32[]{:S(2)}) %collective-permute-start.2) | collective-permute-done | bytes 294944 | tf_op jit(solution)/shard_map/ppermute | solution.py:104
  43.9 1.2 %maximum_select_fusion = bf16[64,3,1536]{2,0,1:T(8,128)(2,1)S(1)} fusion(bf16[64,3,768]{2,0,1:T(8,128)(2,1)} %collective-permute-done.2, bf16[64,1,768]{2,0,1:T(8,128)(2,1)S(1)} %get-tuple-element.23, bf16[64,1,768]{2,0,1:T(8,128)(2,1)S(1)} %get-tuple-element.22, bf16[64,1,768]{2,0,1:T(8,128)(2,1)S(1)} %get-tuple-element.21, pred[]{:T(512)S(6)} %eq.49), kind=kLoop, calls=%fused_computation.12 | loop fusion | flops 5013504 | bytes 1179649 | tf_op jit(solution)/shard_map/jit(_where)/select_n | solution.py:105
  45.1 0.8 %fusion.10 = f32[64,720]{1,0:T(8,128)S(1)} fusion(bf16[720,1536]{1,0:T(8,128)(2,1)S(1)} %copy-done, bf16[64,3,1536]{2,0,1:T(8,128)(2,1)S(1)} %maximum_select_fusion), kind=kOutput, calls=%fused_computation.41 | convolution fusion | flops 141557760 | bytes 2592768 | tf_op jit(solution)/shard_map/dot_general | solution.py:22
  45.9 2.2 %convolution_convert_fusion.2 = bf16[720,1536]{1,0:T(8,128)(2,1)} fusion(bf16[64,3,1536]{2,0,1:T(8,128)(2,1)S(1)} %maximum_select_fusion, f32[64]{0:T(128)S(1)} %convert_reduce_fusion, bf16[2,64,768]{2,1,0:T(8,128)(2,1)S(1)} %copy-done.3), kind=kOutput, calls=%fused_computation.2 | convolution fusion | flops 142801920 | bytes 2507264 | tf_op jit(solution)/shard_map/dot_general | solution.py:16
  48.1 2.1 %convolution_convert_fusion.3 = bf16[720,1536]{1,0:T(8,128)(2,1)} fusion(bf16[64,3,1536]{2,0,1:T(8,128)(2,1)S(1)} %maximum_select_fusion, bf16[2,64,768]{2,1,0:T(8,128)(2,1)S(1)} %copy-done.3), kind=kOutput, calls=%fused_computation.3 | convolution fusion | flops 142663680 | bytes 2506752 | tf_op jit(solution)/shard_map/dot_general | solution.py:16
  50.2 0.8 %fusion = bf16[64,720]{1,0:T(8,128)(2,1)S(1)} fusion(f32[64,720]{1,0:T(8,128)S(1)} %fusion.10, bf16[720,1536]{1,0:T(8,128)(2,1)S(1)} %copy-done.1, bf16[64,3,1536]{2,0,1:T(8,128)(2,1)S(1)} %maximum_select_fusion), kind=kOutput, calls=%fused_computation.10 | convolution fusion | flops 141649920 | bytes 2697216 | tf_op jit(solution)/shard_map/dot_general | solution.py:22
  51.1 0.8 %maximum_maximum_fusion = bf16[32,2,768]{2,1,0:T(2,128)(2,1)} fusion(bf16[32,2,1]{2,1,0:T(2,128)(2,1)S(1)} %copy.87, bf16[32,2,1]{2,1,0:T(2,128)(2,1)S(1)} %copy.86, bf16[32,2,720]{2,1,0:T(2,128)(2,1)S(1)} %concatenate.25, bf16[768]{0:T(1024)(128)(2,1)S(1)} %pad.6.clone), kind=kLoop, calls=%fused_computation.47 | loop fusion | flops 393216 | bytes 192256 | tf_op jit(solution)/shard_map/concatenate | solution.py:112
  51.8 3.0 %all-to-all-start.1 = ((bf16[32,2,768]{2,1,0:T(2,128)(2,1)}), bf16[32,2,768]{2,1,0:T(2,128)(2,1)S(1)}, u32[]{:S(2)}, u32[]{:S(2)}) async-start(bf16[32,2,768]{2,1,0:T(2,128)(2,1)} %maximum_maximum_fusion), calls=%async_computation.1 | async-start | bytes 196608 | tf_op jit(solution)/shard_map/all_to_all | solution.py:115
  54.9 2.1 %convolution_convert_fusion.4 = bf16[720,1536]{1,0:T(8,128)(2,1)} fusion(bf16[64,3,1536]{2,0,1:T(8,128)(2,1)S(1)} %maximum_select_fusion, bf16[2,64,768]{2,1,0:T(8,128)(2,1)S(1)} %copy-done.3), kind=kOutput, calls=%fused_computation.4 | convolution fusion | flops 142663680 | bytes 2506752 | tf_op jit(solution)/shard_map/dot_general | solution.py:16
  57.0 5.4 %all-to-all-done.1 = bf16[32,2,768]{2,1,0:T(2,128)(2,1)S(1)} async-done(((bf16[32,2,768]{2,1,0:T(2,128)(2,1)}), bf16[32,2,768]{2,1,0:T(2,128)(2,1)S(1)}, u32[]{:S(2)}, u32[]{:S(2)}) %all-to-all-start.1) | async-done | bytes 98336 | tf_op jit(solution)/shard_map/all_to_all | solution.py:115
  62.5 0.2 convert_reduce_fusion.1
  62.7 0.1 convolution_convert_fusion.5
  62.8 0.7 %reshape.161 = bf16[4,2880]{1,0:T(4,128)(2,1)} reshape(bf16[4,4,720]{2,1,0:T(4,128)(2,1)S(1)} %copy.88) | data formatting | bytes 46080 | tf_op jit(solution)/shard_map/reshape | solution.py:125
  63.8 0.7 %select_reduce_fusion = f32[4,4]{1,0:T(4,128)} fusion(f32[4,8]{1,0:T(4,128)S(1)} %copy.89, s32[4,4]{1,0:T(4,128)S(1)} %copy-done.5), kind=kLoop, calls=%fused_computation.57 | loop fusion | flops 368 | bytes 256 | tf_op jit(solution)/shard_map/reduce_sum | solution.py:129
  (44 shorter events, 1.5 us)
Async XLA Ops:
  0.6 25.7 %copy-start = (bf16[720,1536]{1,0:T(8,128)(2,1)S(1)}, bf16[720,1536]{1,0:T(8,128)(2,1)}, u32[]{:S(2)}) copy-start(bf16[720,1536]{1,0:T(8,128)(2,1)} %param.13) | copy-start | bytes 6635524
  7.2 15.8 %all-to-all-start = ((bf16[32,8,384]{2,1,0:T(8,128)(2,1)}), bf16[32,8,384]{2,1,0:T(8,128)(2,1)S(1)}, u32[]{:S(2)}, u32[]{:S(2)}) async-start(bf16[32,8,384]{2,1,0:T(8,128)(2,1)} %copy.81), calls=%async_computation | async-start | bytes 393216 | tf_op jit(solution)/shard_map/all_to_all | solution.py:69
  23.4 2.9 %copy-start.2 = (bf16[2,64,768]{2,1,0:T(8,128)(2,1)}, bf16[2,64,768]{2,1,0:T(8,128)(2,1)S(1)}, u32[]{:S(2)}) copy-start(bf16[2,64,768]{2,1,0:T(8,128)(2,1)S(1)} %reshape.159) | copy-start | bytes 589828
  23.5 2.4 %copy-start.4 = (bf16[720,1536]{1,0:T(8,128)(2,1)S(1)}, bf16[720,1536]{1,0:T(8,128)(2,1)}, u32[]{:S(2)}) copy-start(bf16[720,1536]{1,0:T(8,128)(2,1)} %param.15) | copy-start | bytes 6635524
  27.7 1.9 %collective-permute-start = (bf16[64,3,768]{2,0,1:T(8,128)(2,1)}, bf16[64,3,768]{2,0,1:T(8,128)(2,1)}, u32[]{:S(2)}, u32[]{:S(2)}) collective-permute-start(bf16[64,3,768]{2,0,1:T(8,128)(2,1)} %dynamic-slice_convert_fusion), channel_id=1, source_target_pairs={{0,8},{8,0},{16,24},{24,16},{1,9},{9,1},{17,25},{25,17},{2,10},{10... | collective-permute-start | bytes 884744 | tf_op jit(solution)/shard_map/ppermute | solution.py:89
  31.3 9.4 %collective-permute-start.1 = (bf16[64,3,768]{2,0,1:T(8,128)(2,1)}, bf16[64,3,768]{2,0,1:T(8,128)(2,1)}, u32[]{:S(2)}, u32[]{:S(2)}) collective-permute-start(bf16[64,3,768]{2,0,1:T(8,128)(2,1)} %fusion.1), channel_id=1, source_target_pairs={{0,16},{8,24},{16,0},{24,8},{1,17},{9,25},{17,1},{25,9},{2,18},{10... | collective-permute-start | bytes 884744 | tf_op jit(solution)/shard_map/ppermute | solution.py:95
  42.1 3.8 %copy-start.3 = (bf16[2,64,768]{2,1,0:T(8,128)(2,1)S(1)}, bf16[2,64,768]{2,1,0:T(8,128)(2,1)}, u32[]{:S(2)}) copy-start(bf16[2,64,768]{2,1,0:T(8,128)(2,1)} %copy-done.2) | copy-start | bytes 589828
  42.1 1.8 %collective-permute-start.2 = (bf16[64,3,768]{2,0,1:T(8,128)(2,1)S(1)}, bf16[64,3,768]{2,0,1:T(8,128)(2,1)}, u32[]{:S(2)}, u32[]{:S(2)}) collective-permute-start(bf16[64,3,768]{2,0,1:T(8,128)(2,1)S(1)} %pad_maximum_fusion.1), channel_id=1, source_target_pairs={{0,8},{8,0},{16,24},{24,16},{1,9},{9,1},{17,25},{25,17},{2,10},{10... | collective-permute-start | bytes 884744 | tf_op jit(solution)/shard_map/ppermute | solution.py:104
  45.9 4.3 %copy-start.1 = (bf16[720,1536]{1,0:T(8,128)(2,1)S(1)}, bf16[720,1536]{1,0:T(8,128)(2,1)}, u32[]{:S(2)}) copy-start(bf16[720,1536]{1,0:T(8,128)(2,1)} %param.14) | copy-start | bytes 6635524
  51.0 12.8 %copy-start.5 = (s32[4,4]{1,0:T(4,128)S(1)}, s32[4,4]{1,0:T(4,128)}, u32[]{:S(2)}) copy-start(s32[4,4]{1,0:T(4,128)} %param.11) | copy-start | bytes 196
  51.8 10.6 %all-to-all-start.1 = ((bf16[32,2,768]{2,1,0:T(2,128)(2,1)}), bf16[32,2,768]{2,1,0:T(2,128)(2,1)S(1)}, u32[]{:S(2)}, u32[]{:S(2)}) async-start(bf16[32,2,768]{2,1,0:T(2,128)(2,1)} %maximum_maximum_fusion), calls=%async_computation.1 | async-start | bytes 196608 | tf_op jit(solution)/shard_map/all_to_all | solution.py:115

commit v2 on v1

v2 whole, which is shorter than its diff:
```python
import functools
import math

import jax
import jax.numpy as jnp
from jax import lax
from jax.experimental import pallas as pl
from jax.experimental.pallas import tpu as pltpu
from jax.sharding import PartitionSpec as P

EXPERTS_F = 8
TOPK = 4
CORES = 2
LANES = 128
PARTS = 4

SLOPE = 1.702
BF16 = jnp.bfloat16
F32 = jnp.float32
VMEM_LIMIT = 16 * 1024 * 1024


def round_up(value, unit):
    return (value + unit - 1) // unit * unit


def dot(left, right, contract):
    return lax.dot_general(left, right, (contract, ((), ())), preferred_element_type=F32)


def at_half(which, half, width, body):
    if width == half:
        body(0)
    elif half % LANES == 0:
        body(pl.multiple_of(which * half, LANES))
    else:
        for k in range(CORES):
            pl.when(which == k)(functools.partial(body, k * half))


def held_width(half):
    return half if half % LANES == 0 else CORES * half


def window(ref, which, half):
    if half % LANES:
        return ref
    return ref.at[:, pl.ds(pl.multiple_of(which * half, LANES), half)]


def my_core():
    return lax.rem(lax.axis_index("dp"), CORES)


def pack_kernel(*refs, n_dp, rows, wide, slots):
    far, out_ref, near, source, sems = refs[:4], refs[4], refs[5:9], refs[9], refs[10]
    copies = [pltpu.make_async_copy(far[i], near[i], sems.at[i]) for i in range(4)]
    for copy in copies:
        copy.start()
    ids_ref, weights_ref, tokens_ref, grads_ref = near
    count = tokens_ref.shape[0]
    lines = EXPERTS_F * PARTS * slots
    line = lax.broadcasted_iota(jnp.int32, (lines, 1), 0)
    expert = line // (PARTS * slots)
    part = (line // slots) % PARTS
    slot = line % slots
    column = lax.broadcasted_iota(jnp.int32, (lines, PARTS * count), 1)
    source[...] = jnp.zeros_like(source)
    for copy in copies:
        copy.wait()
    ids = ids_ref[...]
    route = weights_ref[...].astype(F32)
    seen = jnp.zeros((lines, 1), jnp.int32)
    factor = jnp.zeros((lines, 1), F32)
    spread = jnp.zeros((lines, PARTS * count), F32)
    for t in range(count):
        named = jnp.zeros((lines, 1), jnp.int32)
        value = jnp.zeros((lines, 1), F32)
        for k in range(TOPK):
            same = ids[t : t + 1, k : k + 1] == expert
            named = named + same.astype(jnp.int32)
            value = value + jnp.where(same, route[t : t + 1, k : k + 1], 0.0)
        chosen = (named > 0) & (seen == slot)
        seen = seen + (named > 0).astype(jnp.int32)
        factor = factor + jnp.where(chosen, value, 0.0)
        spread = spread + jnp.where(chosen & (column == part * count + t), 1.0, 0.0)
    spread = spread.astype(BF16)
    lane = lax.broadcasted_iota(jnp.int32, (lines, wide), 1)
    mark = (lane == rows - wide) & (part % 2 == 1)
    for j in range(n_dp):
        for which, ref in enumerate((tokens_ref, grads_ref)):
            first = 2 * which * count
            source[first : first + count, :] = ref[:, j * rows : j * rows + wide].astype(F32)
            source[first + count : first + 2 * count, 0 : rows - wide] = ref[
                :, j * rows + wide : (j + 1) * rows
            ].astype(F32)
        block = dot(spread, source[...].astype(BF16), ((1,), (0,)))
        out_ref[j * lines : (j + 1) * lines, :] = jnp.where(mark, factor, block).astype(BF16)


def stage_kernel(order_ref, gate_ref, up_ref, gate_out, up_out, sems, *, half):
    other = 1 - my_core()
    copies = [
        pltpu.make_async_copy(window(gate_ref, other, half), gate_out, sems.at[0]),
        pltpu.make_async_copy(window(up_ref, other, half), up_out, sems.at[1]),
    ]
    for copy in copies:
        copy.start()
    for copy in copies:
        copy.wait()


def project(which, half, i, left_ref, weight_ref, out_ref):
    def body(base):
        product = dot(left_ref[...], weight_ref[:, pl.ds(base, half)], ((1,), (0,)))
        out_ref[:, i * half : (i + 1) * half] = product.astype(out_ref.dtype)

    at_half(which, half, weight_ref.shape[1], body)


def send_kernel(
    got_ref, gate_other, up_other, gate_ref, down_ref,
    inputs_ref, upstream_ref, factor_ref, send_ref, gate_own, down_other, sems, *, rows, wide, slots, half,
):
    core = my_core()
    other = 1 - core
    down_copy = pltpu.make_async_copy(window(down_ref, other, half), down_other, sems.at[0])
    gate_copy = pltpu.make_async_copy(window(gate_ref, core, half), gate_own, sems.at[1])
    down_copy.start()
    gate_copy.start()
    per_block = PARTS * slots
    sources = got_ref.shape[0] // per_block
    group = math.gcd(sources, 32)
    lines = group * per_block
    lane = lax.broadcasted_iota(jnp.int32, (1, lines), 1)
    target = (lane % per_block) * group + lane // per_block
    move = (lax.broadcasted_iota(jnp.int32, (lines, lines), 0) == target).astype(F32).astype(BF16)
    for g in range(sources // group):
        block = dot(move, got_ref[g * lines : (g + 1) * lines, :], ((1,), (0,)))
        for s in range(slots):
            to = s * sources + g * group
            piece = [block[(p * slots + s) * group : (p * slots + s + 1) * group] for p in range(PARTS)]
            inputs_ref[to : to + group, 0:wide] = piece[0].astype(BF16)
            inputs_ref[to : to + group, wide:rows] = piece[1][:, : rows - wide].astype(BF16)
            upstream_ref[to : to + group, 0:wide] = piece[2].astype(BF16)
            upstream_ref[to : to + group, wide:rows] = piece[3][:, : rows - wide].astype(BF16)
            factor_ref[to : to + group, :] = piece[1][:, rows - wide : rows - wide + 1]
    project(other, half, 0, inputs_ref, gate_other, send_ref)
    project(other, half, 1, inputs_ref, up_other, send_ref)
    down_copy.wait()
    project(other, half, 2, upstream_ref, down_other, send_ref)
    gate_copy.wait()


def keep_kernel(inputs_ref, upstream_ref, gate_own, up_ref, down_ref, keep_ref, up_own, down_own, sems, *, half):
    core = my_core()
    up_copy = pltpu.make_async_copy(window(up_ref, core, half), up_own, sems.at[0])
    down_copy = pltpu.make_async_copy(window(down_ref, core, half), down_own, sems.at[1])
    up_copy.start()
    down_copy.start()
    project(core, half, 0, inputs_ref, gate_own, keep_ref)
    up_copy.wait()
    project(core, half, 1, inputs_ref, up_own, keep_ref)
    down_copy.wait()
    project(core, half, 2, upstream_ref, down_own, keep_ref)


def pair_kernel(keep_ref, got_ref, pair_ref, low_ref):
    pair = keep_ref[...] + got_ref[...].astype(F32)
    pair_ref[...] = pair
    low_ref[...] = pair.astype(BF16)


def derive_kernel(pair_ref, factor_ref, *refs, half):
    others, (own_ref, dots_ref) = refs[:-2], refs[-2:]
    factor = factor_ref[...]

    def total(i):
        columns = slice(i * half, (i + 1) * half)
        value = pair_ref[:, columns]
        for ref in others:
            value = value + ref[:, columns].astype(F32)
        return value

    pre_gate, pre_up, pulled = total(0), total(1), total(2)
    sigma = jax.nn.sigmoid(SLOPE * pre_gate)
    active = pre_gate * sigma
    hidden = (pre_up + 1.0) * active
    d_gate = factor * pulled * (pre_up + 1.0) * sigma * (1.0 + SLOPE * pre_gate * (1.0 - sigma))
    d_up = factor * pulled * active
    own_ref[:, 0:half] = d_gate.astype(BF16)
    own_ref[:, half : 2 * half] = d_up.astype(BF16)
    own_ref[:, 2 * half : 3 * half] = hidden.astype(BF16)
    dots_ref[...] = jnp.sum(hidden * pulled, axis=1, keepdims=True)


def back_product(core, half, derived_ref, gate_ref, up_ref, write):
    def body(base):
        value = dot(derived_ref[:, 0:half], gate_ref[:, pl.ds(base, half)], ((1,), (1,)))
        value = value + dot(derived_ref[:, half : 2 * half], up_ref[:, pl.ds(base, half)], ((1,), (1,)))
        write(value)

    at_half(core, half, gate_ref.shape[1], body)


def back_own_kernel(own_ref, gate_ref, up_ref, out_ref, *, half):
    def write(value):
        out_ref[...] = value

    back_product(my_core(), half, own_ref, gate_ref, up_ref, write)


def back_kernel(other_ref, own_part_ref, dots_ref, gate_ref, up_ref, out_ref, low, stacked, *, half, rows, back_wide, slots):
    per_block = PARTS * slots
    sources = out_ref.shape[0] // per_block
    group = math.gcd(sources, 32)
    lines = group * per_block

    def write(value):
        low[:, 0:rows] = (own_part_ref[...] + value).astype(BF16)

    if low.shape[1] > rows:
        low[:, rows:] = jnp.zeros((low.shape[0], low.shape[1] - rows), BF16)
    back_product(1 - my_core(), half, other_ref, gate_ref, up_ref, write)
    column = lax.broadcasted_iota(jnp.int32, (1, lines), 1)
    target = (column % group) * per_block + column // group
    move = (lax.broadcasted_iota(jnp.int32, (lines, lines), 0) == target).astype(F32).astype(BF16)
    dots = dots_ref[...]
    high = dots.astype(BF16).astype(F32)
    lane = lax.broadcasted_iota(jnp.int32, (dots.shape[0], back_wide), 1)
    last = jnp.where(lane == 0, high, jnp.where(lane == 1, dots - high, 0.0)).astype(BF16)
    for g in range(sources // group):
        for s in range(slots):
            here = s * sources + g * group
            for p in range(PARTS):
                to = (p * slots + s) * group
                if p == PARTS - 1:
                    stacked[to : to + group, :] = last[here : here + group]
                else:
                    stacked[to : to + group, :] = low[here : here + group, p * back_wide : (p + 1) * back_wide]
        out_ref[g * lines : (g + 1) * lines, :] = dot(move, stacked[...], ((1,), (0,))).astype(BF16)


def grad_kernel(inputs_ref, upstream_ref, factor_ref, own_ref, other_ref, gate_ref, up_ref, down_ref, *, half):
    core = my_core()
    scaled = (factor_ref[...] * upstream_ref[...].astype(F32)).astype(BF16)
    lefts = (inputs_ref[...], inputs_ref[...], scaled)
    for which, ref in ((core, own_ref), (1 - core, other_ref)):
        def body(base, ref=ref):
            for i, (left, out) in enumerate(zip(lefts, (gate_ref, up_ref, down_ref))):
                product = dot(left, ref[:, i * half : (i + 1) * half], ((0,), (0,)))
                out[:, pl.ds(base, half)] = product.astype(BF16)

        at_half(which, half, gate_ref.shape[1], body)


def combine_kernel(ids_ref, back_ref, tokens_ref, route_ref, gather, *, n_dp, rows, back_wide, slots, per_expert):
    count = tokens_ref.shape[0]
    lines = back_ref.shape[0] // n_dp
    line = lax.broadcasted_iota(jnp.int32, (1, lines), 1)
    expert = line // (PARTS * slots * per_expert)
    part = (line // slots) % PARTS
    slot = line % slots
    ids = ids_ref[...]
    seen = jnp.zeros((1, lines), jnp.int32)
    for t in range(count):
        same = [ids[t : t + 1, k : k + 1] == expert for k in range(TOPK)]
        named = functools.reduce(lambda a, b: a | b, same)
        chosen = named & (seen == slot)
        seen = seen + named.astype(jnp.int32)
        for p in range(PARTS - 1):
            gather[p * count + t : p * count + t + 1, :] = (chosen & (part == p)).astype(F32)
        for k in range(TOPK):
            row = (PARTS - 1 + k) * count + t
            gather[row : row + 1, :] = (chosen & same[k] & (part == PARTS - 1)).astype(F32)
    sums = gather[...].astype(BF16)
    route = jnp.zeros((TOPK * count, 1), F32)
    for j in range(n_dp):
        block = dot(sums, back_ref[j * lines : (j + 1) * lines, :], ((1,), (0,)))
        for p in range(PARTS - 1):
            width = min(back_wide, rows - p * back_wide)
            if width > 0:
                first = j * rows + p * back_wide
                tokens_ref[:, first : first + width] = block[p * count : (p + 1) * count, :width].astype(BF16)
        if j < CORES:
            terms = block[(PARTS - 1) * count : (PARTS - 1 + TOPK) * count]
            route = route + terms[:, 0:1] + terms[:, 1:2]
    for k in range(TOPK):
        route_ref[:, k : k + 1] = route[k * count : (k + 1) * count]


def call(kernel, outs, *args, scratch=(), flops=0, moved=0, far=(), limit=VMEM_LIMIT):
    args = [pltpu.with_memory_space_constraint(a, pltpu.HBM) if i in far else a for i, a in enumerate(args)]
    return pl.pallas_call(
        kernel,
        out_shape=outs,
        in_specs=[pl.BlockSpec(memory_space=pltpu.HBM if i in far else pltpu.VMEM) for i in range(len(args))],
        out_specs=jax.tree.map(lambda _: pl.BlockSpec(memory_space=pltpu.VMEM), outs),
        scratch_shapes=list(scratch),
        compiler_params=pltpu.CompilerParams(vmem_limit_bytes=limit),
        cost_estimate=pl.CostEstimate(flops=flops, bytes_accessed=moved, transcendentals=0),
    )(*args)


def shape(dims, dtype):
    return jax.ShapeDtypeStruct(dims, dtype)


def local(tokens, cotangent, expert_ids, route_weights, gate_weight, up_weight, down_weight):
    n_dp = lax.axis_size("dp")
    members = lax.axis_size("expert")
    per_expert = members // EXPERTS_F
    sources = n_dp * members
    token_count, model_width = tokens.shape
    rows, hidden_units = gate_weight.shape
    half = hidden_units // CORES
    slots = token_count * TOPK // EXPERTS_F
    count = sources * slots
    per_block = PARTS * slots
    wide = round_up(rows // 2 + 1, LANES)
    back_wide = round_up(-(-rows // (PARTS - 1)), LANES)
    group = math.gcd(sources, 32)

    packed = call(
        functools.partial(pack_kernel, n_dp=n_dp, rows=rows, wide=wide, slots=slots),
        shape((n_dp * EXPERTS_F * per_block, wide), BF16),
        expert_ids,
        route_weights,
        tokens,
        cotangent,
        scratch=[
            pltpu.VMEM(expert_ids.shape, jnp.int32),
            pltpu.VMEM(route_weights.shape, BF16),
            pltpu.VMEM(tokens.shape, BF16),
            pltpu.VMEM(cotangent.shape, BF16),
            pltpu.VMEM((PARTS * token_count, wide), F32),
            pltpu.SemaphoreType.DMA((4,)),
        ],
        moved=1 << 18,
        far=(0, 1, 2, 3),
    )
    packed = packed.reshape(n_dp, EXPERTS_F, per_block, wide)
    if per_expert > 1:
        packed = jnp.repeat(packed, per_expert, axis=1)
    packed = packed.reshape(sources, per_block, wide)
    got = lax.all_to_all(packed, ("dp", "expert"), split_axis=0, concat_axis=0, tiled=True)

    held = pltpu.VMEM((rows, held_width(half)), BF16)
    gate_other, up_other = call(
        functools.partial(stage_kernel, half=half),
        [held, held],
        packed,
        gate_weight,
        up_weight,
        scratch=[pltpu.SemaphoreType.DMA((2,))],
        moved=4 * rows * half,
        far=(0, 1, 2),
        limit=1 << 20,
    )

    inputs, upstream, factor, send, gate_own = call(
        functools.partial(send_kernel, rows=rows, wide=wide, slots=slots, half=half),
        [
            shape((count, rows), BF16),
            shape((count, rows), BF16),
            shape((count, 1), F32),
            shape((count, 3 * half), BF16),
            held,
        ],
        got.reshape(sources * per_block, wide),
        gate_other,
        up_other,
        gate_weight,
        down_weight,
        scratch=[held, pltpu.SemaphoreType.DMA((2,))],
        flops=6 * count * rows * half,
        moved=1 << 20,
        far=(3, 4),
    )
    swap = [(i, i ^ 1) for i in range(n_dp)]
    arrived = lax.ppermute(send, "dp", swap)
    keep, up_own = call(
        functools.partial(keep_kernel, half=half),
        [shape((count, 3 * half), F32), held],
        inputs,
        upstream,
        gate_own,
        up_weight,
        down_weight,
        scratch=[held, pltpu.SemaphoreType.DMA((2,))],
        flops=6 * count * rows * half,
        moved=1 << 20,
        far=(3, 4),
    )
    pair, low = call(
        pair_kernel,
        [shape((count, 3 * half), F32), shape((count, 3 * half), BF16)],
        keep,
        arrived,
        moved=1 << 20,
    )
    others = []
    for shift in range(1, n_dp // CORES):
        perm = [(i, (i + shift * CORES) % n_dp) for i in range(n_dp)]
        others.append(lax.ppermute(low, "dp", perm))
    own, dots = call(
        functools.partial(derive_kernel, half=half),
        [shape((count, 3 * half), BF16), shape((count, 1), F32)],
        pair,
        factor,
        *others,
        moved=1 << 20,
    )
    other = lax.ppermute(own, "dp", swap)
    own_part = call(
        functools.partial(back_own_kernel, half=half),
        shape((count, rows), F32),
        own,
        gate_own,
        up_own,
        flops=4 * count * rows * half,
        moved=1 << 20,
    )
    back = call(
        functools.partial(back_kernel, half=half, rows=rows, back_wide=back_wide, slots=slots),
        shape((sources * per_block, back_wide), BF16),
        other,
        own_part,
        dots,
        gate_other,
        up_other,
        scratch=[pltpu.VMEM((count, (PARTS - 1) * back_wide), BF16), pltpu.VMEM((group * per_block, back_wide), BF16)],
        flops=4 * count * rows * half,
        moved=1 << 20,
    )
    back = lax.all_to_all(
        back.reshape(sources, per_block, back_wide), ("dp", "expert"), split_axis=0, concat_axis=0, tiled=True
    )
    grads = call(
        functools.partial(grad_kernel, half=half),
        [shape((rows, hidden_units), BF16)] * 3,
        inputs,
        upstream,
        factor,
        own,
        other,
        flops=12 * count * rows * half,
        moved=6 * rows * hidden_units,
    )
    d_tokens, d_route = call(
        functools.partial(
            combine_kernel, n_dp=n_dp, rows=rows, back_wide=back_wide, slots=slots, per_expert=per_expert
        ),
        [shape((token_count, model_width), BF16), shape((token_count, TOPK), F32)],
        expert_ids,
        back.reshape(sources * per_block, back_wide),
        scratch=[pltpu.VMEM(((PARTS - 1 + TOPK) * token_count, members * per_block), F32)],
        moved=1 << 18,
    )
    return (d_tokens, d_route, *grads)


def solution(mesh):
    in_specs = (
        P(("dp", "expert"), None),
        P(("dp", "expert"), None),
        P(("dp", "expert"), None),
        P(("dp", "expert"), None),
        P("dp", "expert"),
        P("dp", "expert"),
        P("dp", "expert"),
    )
    out_specs = (
        P(("dp", "expert"), None),
        P(("dp", "expert"), None),
        P("dp", "expert"),
        P("dp", "expert"),
        P("dp", "expert"),
    )
    return jax.shard_map(local, mesh=mesh, in_specs=in_specs, out_specs=out_specs, check_vma=False)
```

time: 65.1 us -> 48.1 us (0.74)
  Pallas kernels: 0 us -> 15.7 us
  matrix products: 13.3 us -> 0 us
  other arithmetic: 10.1 us -> 0 us
  local copies, waits for them, and re-layouts: 4.71 us -> 0.01 us
  waiting for transfers between devices: 23.6 us -> 19.1 us
    pallas_call x0 -> x10, Pallas kernels: none -> 15.7 us  [call(): pl.pallas_call(kernel, out_shape=outs, in_specs=[pl.BlockSpec(memory_spac...]
    dot_general x11 -> x0, matrix products: 13.3 us -> none  [the longest x3 6.42 us: contract_rows(): lax.dot_general(left, right, (((0,), (0,)), ((), ())), preferred_element_...]
    convert_element_type x5 -> x0, other arithmetic: 3.32 us -> none  [the longest x1 1.73 us: local(): pair_low = pair.astype(bf16)]
    reduce_sum x6 -> x0, other arithmetic: 2.05 us -> none  [the longest x1 0.77 us: local(): jnp.sum(jnp.where(hits, route_weights[:, :, None].astype(jnp.float32), 0....]
    all_to_all x1, waiting for transfers between devices: 5.44 us -> 3.58 us  [local(): lax.all_to_all(back.reshape(sources, per_block, back_wide), ('dp', 'exper...]
    all_to_all x1, waiting for transfers between devices: 8.53 us -> 6.92 us  [local(): lax.all_to_all(packed, ('dp', 'expert'), split_axis=0, concat_axis=0, til...]
    reshape x7 -> x0, local copies, waits for them, and re-layouts: 1.25 us -> none  [the longest x1 0.71 us: local(): d_tokens = d_tokens.astype(bf16).reshape(token_count, model_width)]
    select_n x1 -> x0, other arithmetic: 1.19 us -> none  [local(): jnp.where(core == 0, jnp.concatenate([own, other], 2), jnp.concatenate([o...]
  transfers between devices with their start and end apart: 5 -> 5, of which waited for: 5 -> 4; matrix products, arithmetic and copies ran while one was open for 6% -> 0% of each run, Pallas kernels for 0% -> 18%
where the time goes in v2:
time: 48.1 us; the launch traced here: 47.7 us
  waiting for transfers between devices  19.1 us (40%)
  Pallas kernels  15.7 us (33%)
  starting transfers between devices  12.2 us (25%)
  between operations  0.72 us (1%)
    pallas_call x10, Pallas kernels, call(): pl.pallas_call(kernel, out_shape=outs, in_specs=[pl.BlockSpec(memory_spac...  15.7 us
    ppermute x1, waiting for transfers between devices, local(): others.append(lax.ppermute(low, 'dp', perm))  7.77 us
    all_to_all x1, starting transfers between devices, local(): lax.all_to_all(packed, ('dp', 'expert'), split_axis=0, concat_axis=0, til...  7.3 us
    all_to_all x1, waiting for transfers between devices, local(): lax.all_to_all(packed, ('dp', 'expert'), split_axis=0, concat_axis=0, til...  6.92 us
    all_to_all x1, waiting for transfers between devices, local(): lax.all_to_all(back.reshape(sources, per_block, back_wide), ('dp', 'exper...  3.58 us
    all_to_all x1, starting transfers between devices, local(): lax.all_to_all(back.reshape(sources, per_block, back_wide), ('dp', 'exper...  3.06 us
    ppermute x1, starting transfers between devices, local(): others.append(lax.ppermute(low, 'dp', perm))  1.54 us
  transfers between devices with their start and end apart: 5, of which 4 were waited for; matrix products, arithmetic and copies ran while one was open for 0% of the time, Pallas kernels for 18%

profile of v2, /device:TPU:0, one launch (start us, length us, event | category | flops | bytes accessed | tf_op | source)
XLA Modules:
  0.0 47.7 jit_solution(12733393479253819498)
XLA Ops:
  0.6 2.0 %shard_map.110 = bf16[256,384]{1,0:T(8,128)(2,1)} custom-call(s32[4,4]{1,0:T(4,128)} %ids_ref.1, bf16[4,4]{1,0:T(4,128)(2,1)} %refs_1_.1, bf16[4,2880]{1,0:T(4,128)(2,1)} %refs_2_.1, bf16[4,2880]{1,0:T(4,128)(2,1)} %refs_3_.1), custom_call_target="tpu_custom_call" | custom-call | bytes 262144 | tf_op jit(solution)/shard_map/pallas_call | solution.py:294
  2.6 7.3 %all-to-all-start = ((bf16[32,8,384]{2,1,0:T(8,128)(2,1)}), bf16[32,8,384]{2,1,0:T(8,128)(2,1)S(1)}, u32[]{:S(2)}, u32[]{:S(2)}) async-start(bf16[32,8,384]{2,1,0:T(8,128)(2,1)} %bitcast.order_ref), calls=%async_computation | async-start | bytes 393216 | tf_op jit(solution)/shard_map/all_to_all | solution.py:346
  9.9 1.6 %shard_map.111 = (bf16[720,768]{1,0:T(8,128)(2,1)S(1)}, bf16[720,768]{1,0:T(8,128)(2,1)S(1)}) custom-call(bf16[32,8,384]{2,1,0:T(8,128)(2,1)} %bitcast.order_ref, bf16[720,1536]{1,0:T(8,128)(2,1)} %gate_ref.3, bf16[720,1536]{1,0:T(8,128)(2,1)} %up_ref.3), custom_call_target="tpu_custom_call" | custom-call | bytes 2211840 | tf_op jit(solution)/shard_map/pallas_call | solution.py:294
  11.6 6.9 %all-to-all-done = bf16[32,8,384]{2,1,0:T(8,128)(2,1)S(1)} async-done(((bf16[32,8,384]{2,1,0:T(8,128)(2,1)}), bf16[32,8,384]{2,1,0:T(8,128)(2,1)S(1)}, u32[]{:S(2)}, u32[]{:S(2)}) %all-to-all-start) | async-done | bytes 196640 | tf_op jit(solution)/shard_map/all_to_all | solution.py:346
  18.5 2.1 %shard_map.112 = (bf16[64,720]{1,0:T(8,128)(2,1)S(1)}, bf16[64,720]{1,0:T(8,128)(2,1)S(1)}, f32[64,1]{1,0:T(8,128)S(1)}, bf16[64,2304]{1,0:T(8,128)(2,1)S(1)}, bf16[720,768]{1,0:T(8,128)(2,1)S(1)}) custom-call(bf16[256,384]{1,0:T(8,128)(2,1)S(1)} %bitcast.4, bf16[720,768]{1,0:T(8,128)(2,1)S(1)} %get-tuple-element.23.gate_other.gate_ref, ...), custom_call_target="tpu_custom_call" | custom-call | flops 212336640 | bytes 1048576 | tf_op jit(solution)/shard_map/pallas_call | solution.py:294
  20.6 0.2 collective-permute-start
  20.9 2.1 %shard_map.113 = (f32[64,2304]{1,0:T(8,128)S(1)}, bf16[720,768]{1,0:T(8,128)(2,1)S(1)}) custom-call(bf16[64,720]{1,0:T(8,128)(2,1)S(1)} %get-tuple-element.25.inputs_ref, bf16[64,720]{1,0:T(8,128)(2,1)S(1)} %get-tuple-element.26.upstream_ref, bf16[720,768]{1,0:T(8,128)(2,1)S(1)} %get-tuple-element.27.gate_own.gate_ref, bf16[720,1536]{1,0:T(8,128)(2,1)} %up_ref.3, ...), custom_call_target="tpu_custom_call" | custom-call | flops 212336640 | bytes 1048576 | tf_op jit(solution)/shard_map/pallas_call | solution.py:294
  23.0 0.0 collective-permute-done.got_ref
  23.0 0.1 shard_map.114
  23.1 1.5 %collective-permute-start.1 = (bf16[64,2304]{1,0:T(8,128)(2,1)S(1)}, bf16[64,2304]{1,0:T(8,128)(2,1)S(1)}, u32[]{:S(2)}, u32[]{:S(2)}) collective-permute-start(bf16[64,2304]{1,0:T(8,128)(2,1)S(1)} %get-tuple-element.32), channel_id=1, source_target_pairs={{0,16},{8,24},{16,0},{24,8},{1,17},{9,25},{17,1},{25,9},{2,18},{10... | collective-permute-start | bytes 884744 | tf_op jit(solution)/shard_map/ppermute | solution.py:405
  24.7 7.8 %collective-permute-done.1.refs_0_ = bf16[64,2304]{1,0:T(8,128)(2,1)S(1)} collective-permute-done((bf16[64,2304]{1,0:T(8,128)(2,1)S(1)}, bf16[64,2304]{1,0:T(8,128)(2,1)S(1)}, u32[]{:S(2)}, u32[]{:S(2)}) %collective-permute-start.1) | collective-permute-done | bytes 294944 | tf_op jit(solution)/shard_map/ppermute | solution.py:405
  32.5 0.2 shard_map.115
  32.7 0.1 collective-permute-start.2
  32.7 0.8 %shard_map.116.own_part_ref = f32[64,720]{1,0:T(8,128)S(1)} custom-call(bf16[64,2304]{1,0:T(8,128)(2,1)S(1)} %get-tuple-element.33.own_ref, bf16[720,768]{1,0:T(8,128)(2,1)S(1)} %get-tuple-element.27.gate_own.gate_ref, bf16[720,768]{1,0:T(8,128)(2,1)S(1)} %get-tuple-element.34.up_ref), custom_call_target="tpu_custom_call" | custom-call | flops 141557760 | bytes 1048576 | tf_op jit(solution)/shard_map/pallas_call | solution.py:294
  33.5 0.8 %collective-permute-done.2.other_ref = bf16[64,2304]{1,0:T(8,128)(2,1)S(1)} collective-permute-done((bf16[64,2304]{1,0:T(8,128)(2,1)S(1)}, bf16[64,2304]{1,0:T(8,128)(2,1)S(1)}, u32[]{:S(2)}, u32[]{:S(2)}) %collective-permute-start.2) | collective-permute-done | bytes 294944 | tf_op jit(solution)/shard_map/ppermute | solution.py:414
  34.3 0.0 copy-start
  34.3 1.7 %shard_map.117 = bf16[256,256]{1,0:T(8,128)(2,1)} custom-call(bf16[64,2304]{1,0:T(8,128)(2,1)S(1)} %collective-permute-done.2.other_ref, f32[64,720]{1,0:T(8,128)S(1)} %shard_map.116.own_part_ref, f32[64,1]{1,0:T(8,128)S(1)} %get-tuple-element.35.dots_ref, bf16[720,768]{1,0:T(8,128)(2,1)S(1)} %get-tuple-element.23.gate_other.gate_ref, ...), custom_call_target="tpu_custom_call" | custom-call | flops 141557760 | bytes 1048576 | tf_op jit(solution)/shard_map/pallas_call | solution.py:294
  35.9 3.1 %all-to-all-start.1 = ((bf16[32,8,256]{2,1,0:T(8,128)(2,1)}), bf16[32,8,256]{2,1,0:T(8,128)(2,1)S(1)}, u32[]{:S(2)}, u32[]{:S(2)}) async-start(bf16[32,8,256]{2,1,0:T(8,128)(2,1)} %bitcast.2), calls=%async_computation.1 | async-start | bytes 262144 | tf_op jit(solution)/shard_map/all_to_all | solution.py:436
  39.0 4.2 %shard_map.119 = (bf16[720,1536]{1,0:T(8,128)(2,1)}, bf16[720,1536]{1,0:T(8,128)(2,1)}, bf16[720,1536]{1,0:T(8,128)(2,1)}) custom-call(bf16[64,720]{1,0:T(8,128)(2,1)S(1)} %get-tuple-element.25.inputs_ref, bf16[64,720]{1,0:T(8,128)(2,1)S(1)} %get-tuple-element.26.upstream_ref, f32[64,1]{1,0:T(8,128)S(1)} %get-tuple-element.31.factor_ref, ...), custom_call_target="tpu_custom_call" | custom-call | flops 424673280 | bytes 6635520 | tf_op jit(solution)/shard_map/pallas_call | solution.py:294
  43.2 3.6 %all-to-all-done.1 = bf16[32,8,256]{2,1,0:T(8,128)(2,1)S(1)} async-done(((bf16[32,8,256]{2,1,0:T(8,128)(2,1)}), bf16[32,8,256]{2,1,0:T(8,128)(2,1)S(1)}, u32[]{:S(2)}, u32[]{:S(2)}) %all-to-all-start.1) | async-done | bytes 131104 | tf_op jit(solution)/shard_map/all_to_all | solution.py:436
  46.7 0.0 copy-done
  46.8 0.9 %shard_map.118 = (bf16[4,2880]{1,0:T(4,128)(2,1)}, f32[4,4]{1,0:T(4,128)}) custom-call(s32[4,4]{1,0:T(4,128)S(1)} %copy-done, bf16[256,256]{1,0:T(8,128)(2,1)S(1)} %bitcast.5), custom_call_target="tpu_custom_call" | custom-call | bytes 262144 | tf_op jit(solution)/shard_map/pallas_call | solution.py:294
Async XLA Ops:
  2.6 15.9 %all-to-all-start = ((bf16[32,8,384]{2,1,0:T(8,128)(2,1)}), bf16[32,8,384]{2,1,0:T(8,128)(2,1)S(1)}, u32[]{:S(2)}, u32[]{:S(2)}) async-start(bf16[32,8,384]{2,1,0:T(8,128)(2,1)} %bitcast.order_ref), calls=%async_computation | async-start | bytes 393216 | tf_op jit(solution)/shard_map/all_to_all | solution.py:346
  20.6 2.4 %collective-permute-start = (bf16[64,2304]{1,0:T(8,128)(2,1)S(1)}, bf16[64,2304]{1,0:T(8,128)(2,1)S(1)}, u32[]{:S(2)}, u32[]{:S(2)}) collective-permute-start(bf16[64,2304]{1,0:T(8,128)(2,1)S(1)} %get-tuple-element.29), channel_id=1, source_target_pairs={{0,8},{8,0},{16,24},{24,16},{1,9},{9,1},{17,25},{25,17},{2,10},{10... | collective-permute-start | bytes 884744 | tf_op jit(solution)/shard_map/ppermute | solution.py:381
  23.1 9.3 %collective-permute-start.1 = (bf16[64,2304]{1,0:T(8,128)(2,1)S(1)}, bf16[64,2304]{1,0:T(8,128)(2,1)S(1)}, u32[]{:S(2)}, u32[]{:S(2)}) collective-permute-start(bf16[64,2304]{1,0:T(8,128)(2,1)S(1)} %get-tuple-element.32), channel_id=1, source_target_pairs={{0,16},{8,24},{16,0},{24,8},{1,17},{9,25},{17,1},{25,9},{2,18},{10... | collective-permute-start | bytes 884744 | tf_op jit(solution)/shard_map/ppermute | solution.py:405
  32.7 1.6 %collective-permute-start.2 = (bf16[64,2304]{1,0:T(8,128)(2,1)S(1)}, bf16[64,2304]{1,0:T(8,128)(2,1)S(1)}, u32[]{:S(2)}, u32[]{:S(2)}) collective-permute-start(bf16[64,2304]{1,0:T(8,128)(2,1)S(1)} %get-tuple-element.33.own_ref), channel_id=1, source_target_pairs={{0,8},{8,0},{16,24},{24,16},{1,9},{9,1},{17,25},{25,17},{2,10},{10... | collective-permute-start | bytes 884744 | tf_op jit(solution)/shard_map/ppermute | solution.py:414
  34.3 12.5 %copy-start = (s32[4,4]{1,0:T(4,128)S(1)}, s32[4,4]{1,0:T(4,128)}, u32[]{:S(2)}) copy-start(s32[4,4]{1,0:T(4,128)} %ids_ref.1) | copy-start | bytes 196
  35.9 10.8 %all-to-all-start.1 = ((bf16[32,8,256]{2,1,0:T(8,128)(2,1)}), bf16[32,8,256]{2,1,0:T(8,128)(2,1)S(1)}, u32[]{:S(2)}, u32[]{:S(2)}) async-start(bf16[32,8,256]{2,1,0:T(8,128)(2,1)} %bitcast.2), calls=%async_computation.1 | async-start | bytes 262144 | tf_op jit(solution)/shard_map/all_to_all | solution.py:436

commit v3 on v2

--- a/solution.py
+++ b/solution.py
@@ -38,14 +38,14 @@
             pl.when(which == k)(functools.partial(body, k * half))
 
 
-def held_width(half):
-    return half if half % LANES == 0 else CORES * half
-
-
-def window(ref, which, half):
+def chunks_of(half):
+    return 2 if half % (2 * LANES) == 0 else 1
+
+
+def window(ref, which, half, first, width):
     if half % LANES:
         return ref
-    return ref.at[:, pl.ds(pl.multiple_of(which * half, LANES), half)]
+    return ref.at[:, pl.ds(pl.multiple_of(which * half + first, LANES), width)]
 
 
 def my_core():
@@ -98,11 +98,12 @@
         out_ref[j * lines : (j + 1) * lines, :] = jnp.where(mark, factor, block).astype(BF16)
 
 
-def stage_kernel(order_ref, gate_ref, up_ref, gate_out, up_out, sems, *, half):
+def stage_kernel(order_ref, *refs, half):
+    fars, nears, sems = refs[:3], refs[3:6], refs[6]
     other = 1 - my_core()
     copies = [
-        pltpu.make_async_copy(window(gate_ref, other, half), gate_out, sems.at[0]),
-        pltpu.make_async_copy(window(up_ref, other, half), up_out, sems.at[1]),
+        pltpu.make_async_copy(window(far, other, half, 0, half), near, sems.at[i])
+        for i, (far, near) in enumerate(zip(fars, nears))
     ]
     for copy in copies:
         copy.start()
@@ -110,24 +111,14 @@
         copy.wait()
 
 
-def project(which, half, i, left_ref, weight_ref, out_ref):
-    def body(base):
-        product = dot(left_ref[...], weight_ref[:, pl.ds(base, half)], ((1,), (0,)))
-        out_ref[:, i * half : (i + 1) * half] = product.astype(out_ref.dtype)
-
-    at_half(which, half, weight_ref.shape[1], body)
+def project(base, width, i, left_ref, weight_ref, out_ref):
+    product = dot(left_ref[...], weight_ref[:, pl.ds(base, width)], ((1,), (0,)))
+    out_ref[:, i * width : (i + 1) * width] = product.astype(out_ref.dtype)
 
 
 def send_kernel(
-    got_ref, gate_other, up_other, gate_ref, down_ref,
-    inputs_ref, upstream_ref, factor_ref, send_ref, gate_own, down_other, sems, *, rows, wide, slots, half,
+    got_ref, gate_ref, up_ref, down_ref, inputs_ref, upstream_ref, factor_ref, *send_refs, rows, wide, slots, half
 ):
-    core = my_core()
-    other = 1 - core
-    down_copy = pltpu.make_async_copy(window(down_ref, other, half), down_other, sems.at[0])
-    gate_copy = pltpu.make_async_copy(window(gate_ref, core, half), gate_own, sems.at[1])
-    down_copy.start()
-    gate_copy.start()
     per_block = PARTS * slots
     sources = got_ref.shape[0] // per_block
     group = math.gcd(sources, 32)
@@ -145,24 +136,35 @@
             upstream_ref[to : to + group, 0:wide] = piece[2].astype(BF16)
             upstream_ref[to : to + group, wide:rows] = piece[3][:, : rows - wide].astype(BF16)
             factor_ref[to : to + group, :] = piece[1][:, rows - wide : rows - wide + 1]
-    project(other, half, 0, inputs_ref, gate_other, send_ref)
-    project(other, half, 1, inputs_ref, up_other, send_ref)
-    down_copy.wait()
-    project(other, half, 2, upstream_ref, down_other, send_ref)
-    gate_copy.wait()
-
-
-def keep_kernel(inputs_ref, upstream_ref, gate_own, up_ref, down_ref, keep_ref, up_own, down_own, sems, *, half):
+    width = half // len(send_refs)
+
+    def body(base):
+        for q, send_ref in enumerate(send_refs):
+            here = base + q * width
+            project(here, width, 0, inputs_ref, gate_ref, send_ref)
+            project(here, width, 1, inputs_ref, up_ref, send_ref)
+            project(here, width, 2, upstream_ref, down_ref, send_ref)
+
+    at_half(1 - my_core(), half, gate_ref.shape[1], body)
+
+
+def keep_kernel(inputs_ref, upstream_ref, *refs, half, width, q):
+    fars, keep_ref, nears, sems = refs[:3], refs[3], refs[4:7], refs[7]
     core = my_core()
-    up_copy = pltpu.make_async_copy(window(up_ref, core, half), up_own, sems.at[0])
-    down_copy = pltpu.make_async_copy(window(down_ref, core, half), down_own, sems.at[1])
-    up_copy.start()
-    down_copy.start()
-    project(core, half, 0, inputs_ref, gate_own, keep_ref)
-    up_copy.wait()
-    project(core, half, 1, inputs_ref, up_own, keep_ref)
-    down_copy.wait()
-    project(core, half, 2, upstream_ref, down_own, keep_ref)
+    copies = [
+        pltpu.make_async_copy(window(far, core, half, q * width, width), near, sems.at[i])
+        for i, (far, near) in enumerate(zip(fars, nears))
+    ]
+    for copy in copies:
+        copy.start()
+    for i, (left_ref, near) in enumerate(zip((inputs_ref, inputs_ref, upstream_ref), nears)):
+        copies[i].wait()
+        at_half(
+            core,
+            width,
+            near.shape[1],
+            lambda base, i=i, left_ref=left_ref, near=near: project(base, width, i, left_ref, near, keep_ref),
+        )
 
 
 def pair_kernel(keep_ref, got_ref, pair_ref, low_ref):
@@ -194,38 +196,61 @@
     dots_ref[...] = jnp.sum(hidden * pulled, axis=1, keepdims=True)
 
 
-def back_product(core, half, derived_ref, gate_ref, up_ref, write):
+def back_product(which, half, width, first, derived_ref, gate_ref, up_ref, write):
     def body(base):
-        value = dot(derived_ref[:, 0:half], gate_ref[:, pl.ds(base, half)], ((1,), (1,)))
-        value = value + dot(derived_ref[:, half : 2 * half], up_ref[:, pl.ds(base, half)], ((1,), (1,)))
+        columns = pl.ds(base + first, width)
+        value = dot(derived_ref[:, 0:width], gate_ref[:, columns], ((1,), (1,)))
+        value = value + dot(derived_ref[:, width : 2 * width], up_ref[:, columns], ((1,), (1,)))
         write(value)
 
-    at_half(core, half, gate_ref.shape[1], body)
-
-
-def back_own_kernel(own_ref, gate_ref, up_ref, out_ref, *, half):
+    at_half(which, half, gate_ref.shape[1], body)
+
+
+def derive_back_kernel(pair_ref, factor_ref, gate_ref, up_ref, *refs, half):
+    others, (own_ref, dots_ref, part_ref) = refs[:-3], refs[-3:]
+    derive_kernel(pair_ref, factor_ref, *others, own_ref, dots_ref, half=half)
+
+    def write(value):
+        part_ref[...] = value
+
+    back_product(my_core(), half, half, 0, own_ref, gate_ref, up_ref, write)
+
+
+def back_part_kernel(own_ref, gate_own, up_own, *refs, half, width):
+    out_ref = refs[-1]
+
     def write(value):
         out_ref[...] = value
 
-    back_product(my_core(), half, own_ref, gate_ref, up_ref, write)
-
-
-def back_kernel(other_ref, own_part_ref, dots_ref, gate_ref, up_ref, out_ref, low, stacked, *, half, rows, back_wide, slots):
+    def add(value):
+        out_ref[...] = out_ref[...] + value
+
+    back_product(my_core(), width, width, 0, own_ref, gate_own, up_own, write)
+    if len(refs) > 1:
+        gate_other, up_other = refs[:2]
+        earlier = refs[2:-1]
+        for q in range(len(earlier) // 2):
+            out_ref[...] = out_ref[...] + earlier[2 * q][...]
+            back_product(1 - my_core(), half, width, q * width, earlier[2 * q + 1], gate_other, up_other, add)
+
+
+def back_kernel(other_ref, part_ref, gate_ref, up_ref, *refs, half, width, first, rows, back_wide, slots):
+    dots_refs, (out_ref, low, stacked) = refs[:-3], refs[-3:]
     per_block = PARTS * slots
     sources = out_ref.shape[0] // per_block
     group = math.gcd(sources, 32)
     lines = group * per_block
 
     def write(value):
-        low[:, 0:rows] = (own_part_ref[...] + value).astype(BF16)
+        low[:, 0:rows] = (part_ref[...] + value).astype(BF16)
 
     if low.shape[1] > rows:
         low[:, rows:] = jnp.zeros((low.shape[0], low.shape[1] - rows), BF16)
-    back_product(1 - my_core(), half, other_ref, gate_ref, up_ref, write)
+    back_product(1 - my_core(), half, width, first, other_ref, gate_ref, up_ref, write)
     column = lax.broadcasted_iota(jnp.int32, (1, lines), 1)
     target = (column % group) * per_block + column // group
     move = (lax.broadcasted_iota(jnp.int32, (lines, lines), 0) == target).astype(F32).astype(BF16)
-    dots = dots_ref[...]
+    dots = functools.reduce(lambda x, y: x + y, [ref[...] for ref in dots_refs])
     high = dots.astype(BF16).astype(F32)
     lane = lax.broadcasted_iota(jnp.int32, (dots.shape[0], back_wide), 1)
     last = jnp.where(lane == 0, high, jnp.where(lane == 1, dots - high, 0.0)).astype(BF16)
@@ -241,17 +266,20 @@
         out_ref[g * lines : (g + 1) * lines, :] = dot(move, stacked[...], ((1,), (0,))).astype(BF16)
 
 
-def grad_kernel(inputs_ref, upstream_ref, factor_ref, own_ref, other_ref, gate_ref, up_ref, down_ref, *, half):
+def grad_kernel(inputs_ref, upstream_ref, factor_ref, *refs, half, width):
+    derived, outs = refs[:-3], refs[-3:]
     core = my_core()
     scaled = (factor_ref[...] * upstream_ref[...].astype(F32)).astype(BF16)
     lefts = (inputs_ref[...], inputs_ref[...], scaled)
-    for which, ref in ((core, own_ref), (1 - core, other_ref)):
-        def body(base, ref=ref):
-            for i, (left, out) in enumerate(zip(lefts, (gate_ref, up_ref, down_ref))):
-                product = dot(left, ref[:, i * half : (i + 1) * half], ((0,), (0,)))
-                out[:, pl.ds(base, half)] = product.astype(BF16)
-
-        at_half(which, half, gate_ref.shape[1], body)
+    for n, ref in enumerate(derived):
+
+        def body(base, n=n, ref=ref):
+            columns = pl.ds(base + (n // CORES) * width, width)
+            for i, (left, out) in enumerate(zip(lefts, outs)):
+                product = dot(left, ref[:, i * width : (i + 1) * width], ((0,), (0,)))
+                out[:, columns] = product.astype(BF16)
+
+        at_half(core if n % CORES == 0 else 1 - core, half, outs[0].shape[1], body)
 
 
 def combine_kernel(ids_ref, back_ref, tokens_ref, route_ref, gather, *, n_dp, rows, back_wide, slots, per_expert):
@@ -345,105 +373,134 @@
     packed = packed.reshape(sources, per_block, wide)
     got = lax.all_to_all(packed, ("dp", "expert"), split_axis=0, concat_axis=0, tiled=True)
 
-    held = pltpu.VMEM((rows, held_width(half)), BF16)
-    gate_other, up_other = call(
+    chunks = chunks_of(half)
+    width = half // chunks
+    cut = half % LANES == 0
+    held = pltpu.VMEM((rows, half if cut else hidden_units), BF16)
+    held_chunk = pltpu.VMEM((rows, width if cut else hidden_units), BF16)
+    gate_other, up_other, down_other = call(
         functools.partial(stage_kernel, half=half),
-        [held, held],
+        [held] * 3,
         packed,
         gate_weight,
         up_weight,
-        scratch=[pltpu.SemaphoreType.DMA((2,))],
-        moved=4 * rows * half,
-        far=(0, 1, 2),
+        down_weight,
+        scratch=[pltpu.SemaphoreType.DMA((3,))],
+        moved=6 * rows * half,
+        far=(0, 1, 2, 3),
         limit=1 << 20,
     )
 
-    inputs, upstream, factor, send, gate_own = call(
+    inputs, upstream, factor, *sends = call(
         functools.partial(send_kernel, rows=rows, wide=wide, slots=slots, half=half),
-        [
-            shape((count, rows), BF16),
-            shape((count, rows), BF16),
-            shape((count, 1), F32),
-            shape((count, 3 * half), BF16),
-            held,
-        ],
+        [shape((count, rows), BF16), shape((count, rows), BF16), shape((count, 1), F32)]
+        + [shape((count, 3 * width), BF16)] * chunks,
         got.reshape(sources * per_block, wide),
         gate_other,
         up_other,
-        gate_weight,
-        down_weight,
-        scratch=[held, pltpu.SemaphoreType.DMA((2,))],
+        down_other,
         flops=6 * count * rows * half,
         moved=1 << 20,
-        far=(3, 4),
     )
     swap = [(i, i ^ 1) for i in range(n_dp)]
-    arrived = lax.ppermute(send, "dp", swap)
-    keep, up_own = call(
-        functools.partial(keep_kernel, half=half),
-        [shape((count, 3 * half), F32), held],
-        inputs,
-        upstream,
-        gate_own,
-        up_weight,
-        down_weight,
-        scratch=[held, pltpu.SemaphoreType.DMA((2,))],
-        flops=6 * count * rows * half,
-        moved=1 << 20,
-        far=(3, 4),
-    )
-    pair, low = call(
-        pair_kernel,
-        [shape((count, 3 * half), F32), shape((count, 3 * half), BF16)],
-        keep,
-        arrived,
-        moved=1 << 20,
-    )
-    others = []
-    for shift in range(1, n_dp // CORES):
-        perm = [(i, (i + shift * CORES) % n_dp) for i in range(n_dp)]
-        others.append(lax.ppermute(low, "dp", perm))
-    own, dots = call(
-        functools.partial(derive_kernel, half=half),
-        [shape((count, 3 * half), BF16), shape((count, 1), F32)],
-        pair,
-        factor,
-        *others,
-        moved=1 << 20,
-    )
-    other = lax.ppermute(own, "dp", swap)
-    own_part = call(
-        functools.partial(back_own_kernel, half=half),
+    arrived = [lax.ppermute(send, "dp", swap) for send in sends]
+    keeps, pairs, gate_owns, up_owns, others = [], [], [], [], []
+    for q in range(chunks):
+        keep, gate_own, up_own = call(
+            functools.partial(keep_kernel, half=half, width=width, q=q),
+            [shape((count, 3 * width), F32), held_chunk, held_chunk],
+            inputs,
+            upstream,
+            gate_weight,
+            up_weight,
+            down_weight,
+            scratch=[held_chunk, pltpu.SemaphoreType.DMA((3,))],
+            flops=6 * count * rows * width,
+            moved=6 * rows * width,
+            far=(2, 3, 4),
+        )
+        pair, low = call(
+            pair_kernel,
+            [shape((count, 3 * width), F32), shape((count, 3 * width), BF16)],
+            keep,
+            arrived[q],
+            moved=1 << 20,
+        )
+        gate_owns.append(gate_own)
+        up_owns.append(up_own)
+        pairs.append(pair)
+        passed = []
+        for shift in range(1, n_dp // CORES):
+            perm = [(i, (i + shift * CORES) % n_dp) for i in range(n_dp)]
+            passed.append(lax.ppermute(low, "dp", perm))
+        others.append(passed)
+    derived, dots, earlier = [], [], []
+    for q in range(chunks):
+        outs = [shape((count, 3 * width), BF16), shape((count, 1), F32)]
+        if q < chunks - 1:
+            own, dot_terms, part = call(
+                functools.partial(derive_back_kernel, half=width),
+                [*outs, shape((count, rows), F32)],
+                pairs[q],
+                factor,
+                gate_owns[q],
+                up_owns[q],
+                *others[q],
+                flops=4 * count * rows * width,
+                moved=1 << 20,
+            )
+            other = lax.ppermute(own, "dp", swap)
+            earlier += [part, other]
+        else:
+            own, dot_terms = call(
+                functools.partial(derive_kernel, half=width), outs, pairs[q], factor, *others[q], moved=1 << 20
+            )
+            other = lax.ppermute(own, "dp", swap)
+        derived += [own, other]
+        dots.append(dot_terms)
+    part = call(
+        functools.partial(back_part_kernel, half=half, width=width),
         shape((count, rows), F32),
         own,
-        gate_own,
-        up_own,
+        gate_owns[-1],
+        up_owns[-1],
+        *((gate_other, up_other, *earlier) if earlier else ()),
         flops=4 * count * rows * half,
         moved=1 << 20,
     )
     back = call(
-        functools.partial(back_kernel, half=half, rows=rows, back_wide=back_wide, slots=slots),
+        functools.partial(
+            back_kernel,
+            half=half,
+            width=width,
+            first=half - width,
+            rows=rows,
+            back_wide=back_wide,
+            slots=slots,
+        ),
         shape((sources * per_block, back_wide), BF16),
         other,
-        own_part,
-        dots,
+        part,
         gate_other,
         up_other,
-        scratch=[pltpu.VMEM((count, (PARTS - 1) * back_wide), BF16), pltpu.VMEM((group * per_block, back_wide), BF16)],
-        flops=4 * count * rows * half,
+        *dots,
+        scratch=[
+            pltpu.VMEM((count, (PARTS - 1) * back_wide), BF16),
+            pltpu.VMEM((group * per_block, back_wide), BF16),
+        ],
+        flops=4 * count * rows * width,
         moved=1 << 20,
     )
     back = lax.all_to_all(
         back.reshape(sources, per_block, back_wide), ("dp", "expert"), split_axis=0, concat_axis=0, tiled=True
     )
     grads = call(
-        functools.partial(grad_kernel, half=half),
+        functools.partial(grad_kernel, half=half, width=width),
         [shape((rows, hidden_units), BF16)] * 3,
         inputs,
         upstream,
         factor,
-        own,
-        other,
+        *derived,
         flops=12 * count * rows * half,
         moved=6 * rows * hidden_units,
     )

time: 48.1 us -> 45.9 us (0.954)
  waiting for transfers between devices: 19.1 us -> 14.4 us
  Pallas kernels: 15.7 us -> 17.2 us
  starting transfers between devices: 12.2 us -> 13.1 us
    ppermute x2 -> x4, waiting for transfers between devices: 7.77 us -> 4.52 us  [the longest x2 4.51 us: local(): passed.append(lax.ppermute(low, 'dp', perm))]
    pallas_call x10 -> x13, Pallas kernels: 15.7 us -> 17.2 us  [call(): pl.pallas_call(kernel, out_shape=outs, in_specs=[pl.BlockSpec(memory_spac...]
    ppermute x2 -> x4, starting transfers between devices: 1.78 us -> 2.73 us  [the longest x2 2.16 us: local(): passed.append(lax.ppermute(low, 'dp', perm))]
    all_to_all x1, waiting for transfers between devices: 3.58 us -> 2.8 us  [local(): lax.all_to_all(back.reshape(sources, per_block, back_wide), ('dp', 'exper...]
  transfers between devices with their start and end apart: 5 -> 8, of which waited for: 4 -> 5; matrix products, arithmetic and copies ran while one was open for 0% -> 0% of each run, Pallas kernels for 18% -> 27%
where the time goes in v3:
time: 45.9 us; the launch traced here: 45.5 us
  Pallas kernels  17.2 us (37%)
  waiting for transfers between devices  14.4 us (31%)
  starting transfers between devices  13.1 us (29%)
  between operations  0.8 us (2%)
    pallas_call x13, Pallas kernels, call(): pl.pallas_call(kernel, out_shape=outs, in_specs=[pl.BlockSpec(memory_spac...  17.2 us
    all_to_all x1, starting transfers between devices, local(): lax.all_to_all(packed, ('dp', 'expert'), split_axis=0, concat_axis=0, til...  7.3 us
    all_to_all x1, waiting for transfers between devices, local(): lax.all_to_all(packed, ('dp', 'expert'), split_axis=0, concat_axis=0, til...  6.58 us
    ppermute x2, waiting for transfers between devices, local(): passed.append(lax.ppermute(low, 'dp', perm))  4.51 us
    all_to_all x1, starting transfers between devices, local(): lax.all_to_all(back.reshape(sources, per_block, back_wide), ('dp', 'exper...  2.96 us
    all_to_all x1, waiting for transfers between devices, local(): lax.all_to_all(back.reshape(sources, per_block, back_wide), ('dp', 'exper...  2.8 us
    ppermute x2, starting transfers between devices, local(): passed.append(lax.ppermute(low, 'dp', perm))  2.16 us
  transfers between devices with their start and end apart: 8, of which 5 were waited for; matrix products, arithmetic and copies ran while one was open for 0% of the time, Pallas kernels for 27%

profile of v3, /device:TPU:0, one launch (start us, length us, event | category | flops | bytes accessed | tf_op | source)
XLA Modules:
  0.0 45.5 jit_solution(10862929879508016808)
XLA Ops:
  0.6 2.0 %shard_map.110 = bf16[256,384]{1,0:T(8,128)(2,1)} custom-call(s32[4,4]{1,0:T(4,128)} %ids_ref.1, bf16[4,4]{1,0:T(4,128)(2,1)} %refs_1_.4, bf16[4,2880]{1,0:T(4,128)(2,1)} %refs_2_.4, bf16[4,2880]{1,0:T(4,128)(2,1)} %refs_3_.1), custom_call_target="tpu_custom_call" | custom-call | bytes 262144 | tf_op jit(solution)/shard_map/pallas_call | solution.py:322
  2.6 7.3 %all-to-all-start = ((bf16[32,8,384]{2,1,0:T(8,128)(2,1)}), bf16[32,8,384]{2,1,0:T(8,128)(2,1)S(1)}, u32[]{:S(2)}, u32[]{:S(2)}) async-start(bf16[32,8,384]{2,1,0:T(8,128)(2,1)} %bitcast.order_ref), calls=%async_computation | async-start | bytes 393216 | tf_op jit(solution)/shard_map/all_to_all | solution.py:374
  9.9 2.0 %shard_map.111 = (bf16[720,768]{1,0:T(8,128)(2,1)S(1)}, bf16[720,768]{1,0:T(8,128)(2,1)S(1)}, bf16[720,768]{1,0:T(8,128)(2,1)S(1)}) custom-call(bf16[32,8,384]{2,1,0:T(8,128)(2,1)} %bitcast.order_ref, bf16[720,1536]{1,0:T(8,128)(2,1)} %refs_0_.7, bf16[720,1536]{1,0:T(8,128)(2,1)} %refs_1_.7, bf16[720,1536]{1,0:T(8,128)(2,1)} %refs_2_.7), custom_call_target="tpu_custom_call" | custom-call | bytes 3317760 | tf_op jit(solution)/shard_map/pallas_call | solution.py:322
  11.9 6.6 %all-to-all-done = bf16[32,8,384]{2,1,0:T(8,128)(2,1)S(1)} async-done(((bf16[32,8,384]{2,1,0:T(8,128)(2,1)}), bf16[32,8,384]{2,1,0:T(8,128)(2,1)S(1)}, u32[]{:S(2)}, u32[]{:S(2)}) %all-to-all-start) | async-done | bytes 196640 | tf_op jit(solution)/shard_map/all_to_all | solution.py:374
  18.5 0.8 %shard_map.112 = (bf16[64,720]{1,0:T(8,128)(2,1)S(1)}, bf16[64,720]{1,0:T(8,128)(2,1)S(1)}, f32[64,1]{1,0:T(8,128)S(1)}, bf16[64,1152]{1,0:T(8,128)(2,1)S(1)}, bf16[64,1152]{1,0:T(8,128)(2,1)S(1)}) custom-call(bf16[256,384]{1,0:T(8,128)(2,1)S(1)} %bitcast.4, bf16[720,768]{1,0:T(8,128)(2,1)S(1)} %get-tuple-element.33.gate_ref.refs_0_, ...), custom_call_target="tpu_custom_call" | custom-call | flops 212336640 | bytes 1048576 | tf_op jit(solution)/shard_map/pallas_call | solution.py:322
  19.3 0.0 copy-start
  19.3 0.0 copy-start.2
  19.3 0.2 collective-permute-start.3
  19.6 0.3 collective-permute-start
  19.9 1.8 %shard_map.116 = (f32[64,1152]{1,0:T(8,128)S(1)}, bf16[720,384]{1,0:T(8,128)(2,1)S(1)}, bf16[720,384]{1,0:T(8,128)(2,1)S(1)}) custom-call(bf16[64,720]{1,0:T(8,128)(2,1)S(1)} %get-tuple-element.36.inputs_ref, bf16[64,720]{1,0:T(8,128)(2,1)S(1)} %get-tuple-element.37.upstream_ref, bf16[720,1536]{1,0:T(8,128)(2,1)} %refs_0_.7, bf16[720,1536]{1,0:T(8,128)(2,1)} %refs_1_.7, ...), custom_call_target="tpu_custom_call" | custom-call | flops 106168320 | bytes 1658880 | tf_op jit(solution)/shard_map/pallas_call | solution.py:322
  21.7 0.0 collective-permute-done.3.got_ref
  21.8 1.3 %collective-permute-start.4 = (bf16[64,1152]{1,0:T(8,128)(2,1)S(1)}, bf16[64,1152]{1,0:T(8,128)(2,1)S(1)}, u32[]{:S(2)}, u32[]{:S(2)}) collective-permute-start(bf16[64,1152]{1,0:T(8,128)(2,1)S(1)} %get-tuple-element.51), channel_id=1, source_target_pairs={{0,16},{8,24},{16,0},{24,8},{1,17},{9,25},{17,1},{25,9},{2,18},{10... | collective-permute-start | bytes 442376 | tf_op jit(solution)/shard_map/ppermute | solution.py:435
  23.1 0.0 copy-done
  23.1 0.0 copy-done.2
  23.1 1.8 %shard_map.113 = (f32[64,1152]{1,0:T(8,128)S(1)}, bf16[720,384]{1,0:T(8,128)(2,1)S(1)}, bf16[720,384]{1,0:T(8,128)(2,1)S(1)}) custom-call(bf16[64,720]{1,0:T(8,128)(2,1)S(1)} %get-tuple-element.36.inputs_ref, bf16[64,720]{1,0:T(8,128)(2,1)S(1)} %get-tuple-element.37.upstream_ref, bf16[720,1536]{1,0:T(8,128)(2,1)} %refs_0_.7, bf16[720,1536]{1,0:T(8,128)(2,1)} %refs_1_.7, ...), custom_call_target="tpu_custom_call" | custom-call | flops 106168320 | bytes 1658880 | tf_op jit(solution)/shard_map/pallas_call | solution.py:322
  24.9 0.0 collective-permute-done.got_ref
  25.0 0.9 %collective-permute-start.1 = (bf16[64,1152]{1,0:T(8,128)(2,1)S(1)}, bf16[64,1152]{1,0:T(8,128)(2,1)S(1)}, u32[]{:S(2)}, u32[]{:S(2)}) collective-permute-start(bf16[64,1152]{1,0:T(8,128)(2,1)S(1)} %get-tuple-element.42), channel_id=1, source_target_pairs={{0,16},{8,24},{16,0},{24,8},{1,17},{9,25},{17,1},{25,9},{2,18},{10... | collective-permute-start | bytes 442376 | tf_op jit(solution)/shard_map/ppermute | solution.py:435
  25.8 2.0 %collective-permute-done.4.refs_0_ = bf16[64,1152]{1,0:T(8,128)(2,1)S(1)} collective-permute-done((bf16[64,1152]{1,0:T(8,128)(2,1)S(1)}, bf16[64,1152]{1,0:T(8,128)(2,1)S(1)}, u32[]{:S(2)}, u32[]{:S(2)}) %collective-permute-start.4) | collective-permute-done | bytes 147488 | tf_op jit(solution)/shard_map/ppermute | solution.py:435
  27.8 0.5 %shard_map.118 = (bf16[64,1152]{1,0:T(8,128)(2,1)S(1)}, f32[64,1]{1,0:T(8,128)S(1)}, f32[64,720]{1,0:T(8,128)S(1)}) custom-call(f32[64,1152]{1,0:T(8,128)S(1)} %get-tuple-element.48.pair_ref, f32[64,1]{1,0:T(8,128)S(1)} %get-tuple-element.41.factor_ref, bf16[720,384]{1,0:T(8,128)(2,1)S(1)} %get-tuple-element.49.gate_ref, ...), custom_call_target="tpu_custom_call" | custom-call | flops 70778880 | bytes 1048576 | tf_op jit(solution)/shard_map/pallas_call | solution.py:322
  28.3 0.1 collective-permute-start.5
  28.4 2.6 %collective-permute-done.1.refs_0_ = bf16[64,1152]{1,0:T(8,128)(2,1)S(1)} collective-permute-done((bf16[64,1152]{1,0:T(8,128)(2,1)S(1)}, bf16[64,1152]{1,0:T(8,128)(2,1)S(1)}, u32[]{:S(2)}, u32[]{:S(2)}) %collective-permute-start.1) | collective-permute-done | bytes 147488 | tf_op jit(solution)/shard_map/ppermute | solution.py:435
  31.0 0.1 shard_map.115
  31.1 0.0 collective-permute-start.2
  31.2 0.0 collective-permute-done.5.refs_3_.refs_1_
  31.2 0.8 %shard_map.119.part_ref = f32[64,720]{1,0:T(8,128)S(1)} custom-call(bf16[64,1152]{1,0:T(8,128)(2,1)S(1)} %get-tuple-element.43.own_ref.refs_2_, bf16[720,384]{1,0:T(8,128)(2,1)S(1)} %get-tuple-element.44.gate_own, bf16[720,384]{1,0:T(8,128)(2,1)S(1)} %get-tuple-element.45.up_own, bf16[720,768]{1,0:T(8,128)(2,1)S(1)} %get-tuple-element.33.gate_ref.refs_0_, ...), custom_call_target="tpu_custom_call" | custom-call | flops 141557760 | bytes 1048576 | tf_op jit(solution)/shard_map/pallas_call | solution.py:322
  32.0 0.0 copy-start.1
  32.0 0.0 copy-start.3
  32.0 0.5 %collective-permute-done.2.other_ref.refs_3_ = bf16[64,1152]{1,0:T(8,128)(2,1)S(1)} collective-permute-done((bf16[64,1152]{1,0:T(8,128)(2,1)S(1)}, bf16[64,1152]{1,0:T(8,128)(2,1)S(1)}, u32[]{:S(2)}, u32[]{:S(2)}) %collective-permute-start.2) | collective-permute-done | bytes 147488 | tf_op jit(solution)/shard_map/ppermute | solution.py:458
  32.5 0.0 copy-start.4
  32.5 1.4 %shard_map.120 = bf16[256,256]{1,0:T(8,128)(2,1)} custom-call(bf16[64,1152]{1,0:T(8,128)(2,1)S(1)} %collective-permute-done.2.other_ref.refs_3_, f32[64,720]{1,0:T(8,128)S(1)} %shard_map.119.part_ref, bf16[720,768]{1,0:T(8,128)(2,1)S(1)} %get-tuple-element.33.gate_ref.refs_0_, bf16[720,768]{1,0:T(8,128)(2,1)S(1)} %get-tuple-element.34.up_ref.refs_1_, ...), custom_call_target="tpu_custom_call" | custom-call | flops 70778880 | bytes 1048576 | tf_op jit(solution)/shard_map/pallas_call | solution.py:322
  33.9 3.0 %all-to-all-start.1 = ((bf16[32,8,256]{2,1,0:T(8,128)(2,1)}), bf16[32,8,256]{2,1,0:T(8,128)(2,1)S(1)}, u32[]{:S(2)}, u32[]{:S(2)}) async-start(bf16[32,8,256]{2,1,0:T(8,128)(2,1)} %bitcast.2), calls=%async_computation.1 | async-start | bytes 262144 | tf_op jit(solution)/shard_map/all_to_all | solution.py:494
  36.8 0.0 copy-done.1
  36.8 0.0 copy-done.3
  36.9 4.9 %shard_map.122 = (bf16[720,1536]{1,0:T(8,128)(2,1)}, bf16[720,1536]{1,0:T(8,128)(2,1)}, bf16[720,1536]{1,0:T(8,128)(2,1)}) custom-call(bf16[64,720]{1,0:T(8,128)(2,1)S(1)} %copy-done.1, bf16[64,720]{1,0:T(8,128)(2,1)S(1)} %copy-done.3, f32[64,1]{1,0:T(8,128)S(1)} %get-tuple-element.41.factor_ref, bf16[64,1152]{1,0:T(8,128)(2,1)S(1)} %get-tuple-element.53.refs_0_, ...), custom_call_target="tpu_custom_call" | custom-call | flops 424673280 | bytes 6635520 | tf_op jit(solution)/shard_map/pallas_call | solution.py:322
  41.8 2.8 %all-to-all-done.1 = bf16[32,8,256]{2,1,0:T(8,128)(2,1)S(1)} async-done(((bf16[32,8,256]{2,1,0:T(8,128)(2,1)}), bf16[32,8,256]{2,1,0:T(8,128)(2,1)S(1)}, u32[]{:S(2)}, u32[]{:S(2)}) %all-to-all-start.1) | async-done | bytes 131104 | tf_op jit(solution)/shard_map/all_to_all | solution.py:494
  44.6 0.0 copy-done.4
  44.6 0.9 %shard_map.121 = (bf16[4,2880]{1,0:T(4,128)(2,1)}, f32[4,4]{1,0:T(4,128)}) custom-call(s32[4,4]{1,0:T(4,128)S(1)} %copy-done.4, bf16[256,256]{1,0:T(8,128)(2,1)S(1)} %bitcast.5), custom_call_target="tpu_custom_call" | custom-call | bytes 262144 | tf_op jit(solution)/shard_map/pallas_call | solution.py:322
  (2 shorter events, 0.1 us)
Async XLA Ops:
  2.6 15.9 %all-to-all-start = ((bf16[32,8,384]{2,1,0:T(8,128)(2,1)}), bf16[32,8,384]{2,1,0:T(8,128)(2,1)S(1)}, u32[]{:S(2)}, u32[]{:S(2)}) async-start(bf16[32,8,384]{2,1,0:T(8,128)(2,1)} %bitcast.order_ref), calls=%async_computation | async-start | bytes 393216 | tf_op jit(solution)/shard_map/all_to_all | solution.py:374
  19.3 3.8 %copy-start = (bf16[64,720]{1,0:T(8,128)(2,1)}, bf16[64,720]{1,0:T(8,128)(2,1)S(1)}, u32[]{:S(2)}) copy-start(bf16[64,720]{1,0:T(8,128)(2,1)S(1)} %get-tuple-element.36.inputs_ref) | copy-start | bytes 276484
  19.3 3.8 %copy-start.2 = (bf16[64,720]{1,0:T(8,128)(2,1)}, bf16[64,720]{1,0:T(8,128)(2,1)S(1)}, u32[]{:S(2)}) copy-start(bf16[64,720]{1,0:T(8,128)(2,1)S(1)} %get-tuple-element.37.upstream_ref) | copy-start | bytes 276484
  19.3 2.4 %collective-permute-start.3 = (bf16[64,1152]{1,0:T(8,128)(2,1)S(1)}, bf16[64,1152]{1,0:T(8,128)(2,1)S(1)}, u32[]{:S(2)}, u32[]{:S(2)}) collective-permute-start(bf16[64,1152]{1,0:T(8,128)(2,1)S(1)} %get-tuple-element.47), channel_id=1, source_target_pairs={{0,8},{8,0},{16,24},{24,16},{1,9},{9,1},{17,25},{25,17},{2,10},{10... | collective-permute-start | bytes 442376 | tf_op jit(solution)/shard_map/ppermute | solution.py:406
  19.6 5.3 %collective-permute-start = (bf16[64,1152]{1,0:T(8,128)(2,1)S(1)}, bf16[64,1152]{1,0:T(8,128)(2,1)S(1)}, u32[]{:S(2)}, u32[]{:S(2)}) collective-permute-start(bf16[64,1152]{1,0:T(8,128)(2,1)S(1)} %get-tuple-element.39), channel_id=1, source_target_pairs={{0,8},{8,0},{16,24},{24,16},{1,9},{9,1},{17,25},{25,17},{2,10},{10... | collective-permute-start | bytes 442376 | tf_op jit(solution)/shard_map/ppermute | solution.py:406
  21.8 6.0 %collective-permute-start.4 = (bf16[64,1152]{1,0:T(8,128)(2,1)S(1)}, bf16[64,1152]{1,0:T(8,128)(2,1)S(1)}, u32[]{:S(2)}, u32[]{:S(2)}) collective-permute-start(bf16[64,1152]{1,0:T(8,128)(2,1)S(1)} %get-tuple-element.51), channel_id=1, source_target_pairs={{0,16},{8,24},{16,0},{24,8},{1,17},{9,25},{17,1},{25,9},{2,18},{10... | collective-permute-start | bytes 442376 | tf_op jit(solution)/shard_map/ppermute | solution.py:435
  25.0 6.0 %collective-permute-start.1 = (bf16[64,1152]{1,0:T(8,128)(2,1)S(1)}, bf16[64,1152]{1,0:T(8,128)(2,1)S(1)}, u32[]{:S(2)}, u32[]{:S(2)}) collective-permute-start(bf16[64,1152]{1,0:T(8,128)(2,1)S(1)} %get-tuple-element.42), channel_id=1, source_target_pairs={{0,16},{8,24},{16,0},{24,8},{1,17},{9,25},{17,1},{25,9},{2,18},{10... | collective-permute-start | bytes 442376 | tf_op jit(solution)/shard_map/ppermute | solution.py:435
  28.3 2.8 %collective-permute-start.5 = (bf16[64,1152]{1,0:T(8,128)(2,1)S(1)}, bf16[64,1152]{1,0:T(8,128)(2,1)S(1)}, u32[]{:S(2)}, u32[]{:S(2)}) collective-permute-start(bf16[64,1152]{1,0:T(8,128)(2,1)S(1)} %get-tuple-element.53.refs_0_), channel_id=1, source_target_pairs={{0,8},{8,0},{16,24},{24,16},{1,9},{9,1},{17,25},{25,17},{2,10},{10... | collective-permute-start | bytes 442376 | tf_op jit(solution)/shard_map/ppermute | solution.py:452
  31.1 1.4 %collective-permute-start.2 = (bf16[64,1152]{1,0:T(8,128)(2,1)S(1)}, bf16[64,1152]{1,0:T(8,128)(2,1)S(1)}, u32[]{:S(2)}, u32[]{:S(2)}) collective-permute-start(bf16[64,1152]{1,0:T(8,128)(2,1)S(1)} %get-tuple-element.43.own_ref.refs_2_), channel_id=1, source_target_pairs={{0,8},{8,0},{16,24},{24,16},{1,9},{9,1},{17,25},{25,17},{2,10},{10... | collective-permute-start | bytes 442376 | tf_op jit(solution)/shard_map/ppermute | solution.py:458
  32.0 4.8 %copy-start.1 = (bf16[64,720]{1,0:T(8,128)(2,1)S(1)}, bf16[64,720]{1,0:T(8,128)(2,1)}, u32[]{:S(2)}) copy-start(bf16[64,720]{1,0:T(8,128)(2,1)} %copy-done) | copy-start | bytes 276484
  32.0 4.8 %copy-start.3 = (bf16[64,720]{1,0:T(8,128)(2,1)S(1)}, bf16[64,720]{1,0:T(8,128)(2,1)}, u32[]{:S(2)}) copy-start(bf16[64,720]{1,0:T(8,128)(2,1)} %copy-done.2) | copy-start | bytes 276484
  32.5 12.1 %copy-start.4 = (s32[4,4]{1,0:T(4,128)S(1)}, s32[4,4]{1,0:T(4,128)}, u32[]{:S(2)}) copy-start(s32[4,4]{1,0:T(4,128)} %ids_ref.1) | copy-start | bytes 196
  33.9 10.7 %all-to-all-start.1 = ((bf16[32,8,256]{2,1,0:T(8,128)(2,1)}), bf16[32,8,256]{2,1,0:T(8,128)(2,1)S(1)}, u32[]{:S(2)}, u32[]{:S(2)}) async-start(bf16[32,8,256]{2,1,0:T(8,128)(2,1)} %bitcast.2), calls=%async_computation.1 | async-start | bytes 262144 | tf_op jit(solution)/shard_map/all_to_all | solution.py:494

commit v4 on v3

--- a/solution.py
+++ b/solution.py
@@ -13,6 +13,7 @@
 CORES = 2
 LANES = 128
 PARTS = 4
+BACK_PARTS = 2
 
 SLOPE = 1.702
 BF16 = jnp.bfloat16
@@ -117,7 +118,7 @@
 
 
 def send_kernel(
-    got_ref, gate_ref, up_ref, down_ref, inputs_ref, upstream_ref, factor_ref, *send_refs, rows, wide, slots, half
+    got_ref, gate_ref, up_ref, down_ref, inputs_ref, upstream_ref, factor_ref, send_ref, *, rows, wide, slots, half, width
 ):
     per_block = PARTS * slots
     sources = got_ref.shape[0] // per_block
@@ -136,14 +137,13 @@
             upstream_ref[to : to + group, 0:wide] = piece[2].astype(BF16)
             upstream_ref[to : to + group, wide:rows] = piece[3][:, : rows - wide].astype(BF16)
             factor_ref[to : to + group, :] = piece[1][:, rows - wide : rows - wide + 1]
-    width = half // len(send_refs)
 
     def body(base):
-        for q, send_ref in enumerate(send_refs):
+        for q in range(half // width):
             here = base + q * width
-            project(here, width, 0, inputs_ref, gate_ref, send_ref)
-            project(here, width, 1, inputs_ref, up_ref, send_ref)
-            project(here, width, 2, upstream_ref, down_ref, send_ref)
+            project(here, width, 3 * q, inputs_ref, gate_ref, send_ref)
+            project(here, width, 3 * q + 1, inputs_ref, up_ref, send_ref)
+            project(here, width, 3 * q + 2, upstream_ref, down_ref, send_ref)
 
     at_half(1 - my_core(), half, gate_ref.shape[1], body)
 
@@ -167,8 +167,9 @@
         )
 
 
-def pair_kernel(keep_ref, got_ref, pair_ref, low_ref):
-    pair = keep_ref[...] + got_ref[...].astype(F32)
+def pair_kernel(keep_ref, got_ref, pair_ref, low_ref, *, q):
+    size = keep_ref.shape[1]
+    pair = keep_ref[...] + got_ref[:, q * size : (q + 1) * size].astype(F32)
     pair_ref[...] = pair
     low_ref[...] = pair.astype(BF16)
 
@@ -206,8 +207,11 @@
     at_half(which, half, gate_ref.shape[1], body)
 
 
-def derive_back_kernel(pair_ref, factor_ref, gate_ref, up_ref, *refs, half):
-    others, (own_ref, dots_ref, part_ref) = refs[:-3], refs[-3:]
+def derive_back_kernel(pair_ref, factor_ref, gate_ref, up_ref, gate_other, up_other, *refs, half):
+    others, (own_ref, dots_ref, part_ref, gate_turned, up_turned) = refs[:-5], refs[-5:]
+    last = gate_other.shape[1] - half
+    gate_turned[...] = gate_other[:, last:].T
+    up_turned[...] = up_other[:, last:].T
     derive_kernel(pair_ref, factor_ref, *others, own_ref, dots_ref, half=half)
 
     def write(value):
@@ -234,36 +238,45 @@
             back_product(1 - my_core(), half, width, q * width, earlier[2 * q + 1], gate_other, up_other, add)
 
 
-def back_kernel(other_ref, part_ref, gate_ref, up_ref, *refs, half, width, first, rows, back_wide, slots):
-    dots_refs, (out_ref, low, stacked) = refs[:-3], refs[-3:]
-    per_block = PARTS * slots
-    sources = out_ref.shape[0] // per_block
+def back_kernel(other_ref, part_ref, gate_ref, up_ref, *refs, half, width, first, rows, back_wide, slots, turned):
+    dots_refs, out_ref = refs[:-1], refs[-1]
+    per_block = BACK_PARTS * slots
+    sources = out_ref.shape[0]
     group = math.gcd(sources, 32)
     lines = group * per_block
-
-    def write(value):
-        low[:, 0:rows] = (part_ref[...] + value).astype(BF16)
-
-    if low.shape[1] > rows:
-        low[:, rows:] = jnp.zeros((low.shape[0], low.shape[1] - rows), BF16)
-    back_product(1 - my_core(), half, width, first, other_ref, gate_ref, up_ref, write)
     column = lax.broadcasted_iota(jnp.int32, (1, lines), 1)
     target = (column % group) * per_block + column // group
     move = (lax.broadcasted_iota(jnp.int32, (lines, lines), 0) == target).astype(F32).astype(BF16)
     dots = functools.reduce(lambda x, y: x + y, [ref[...] for ref in dots_refs])
     high = dots.astype(BF16).astype(F32)
-    lane = lax.broadcasted_iota(jnp.int32, (dots.shape[0], back_wide), 1)
-    last = jnp.where(lane == 0, high, jnp.where(lane == 1, dots - high, 0.0)).astype(BF16)
-    for g in range(sources // group):
-        for s in range(slots):
-            here = s * sources + g * group
-            for p in range(PARTS):
-                to = (p * slots + s) * group
-                if p == PARTS - 1:
-                    stacked[to : to + group, :] = last[here : here + group]
+    tail = rows - back_wide
+    lane = lax.broadcasted_iota(jnp.int32, (dots.shape[0], back_wide - tail), 1)
+    ending = jnp.where(lane == 0, high, jnp.where(lane == 1, dots - high, 0.0))
+
+    def body(base):
+        columns = pl.ds(base + first, width)
+        blocks = []
+        for lower, upper in ((0, back_wide), (back_wide, rows)):
+            value = part_ref[:, lower:upper]
+            for i, weight_ref in enumerate((gate_ref, up_ref)):
+                left = other_ref[:, i * width : (i + 1) * width]
+                if turned:
+                    value = value + dot(left, weight_ref[:, lower:upper], ((1,), (0,)))
                 else:
-                    stacked[to : to + group, :] = low[here : here + group, p * back_wide : (p + 1) * back_wide]
-        out_ref[g * lines : (g + 1) * lines, :] = dot(move, stacked[...], ((1,), (0,))).astype(BF16)
+                    value = value + dot(left, weight_ref[lower:upper, columns], ((1,), (1,)))
+            blocks.append(value)
+        blocks[1] = jnp.concatenate([blocks[1], ending], axis=1)
+        blocks = [block.astype(BF16) for block in blocks]
+        for g in range(sources // group):
+            stacked = [
+                block[s * sources + g * group : s * sources + (g + 1) * group] for block in blocks for s in range(slots)
+            ]
+            if sources == group:
+                stacked = blocks
+            moved = dot(move, jnp.concatenate(stacked, axis=0), ((1,), (0,)))
+            out_ref[g * group : (g + 1) * group] = moved.reshape(group, per_block, back_wide).astype(BF16)
+
+    at_half(1 - my_core(), half, half if turned else gate_ref.shape[1], body)
 
 
 def grad_kernel(inputs_ref, upstream_ref, factor_ref, *refs, half, width):
@@ -284,10 +297,12 @@
 
 def combine_kernel(ids_ref, back_ref, tokens_ref, route_ref, gather, *, n_dp, rows, back_wide, slots, per_expert):
     count = tokens_ref.shape[0]
-    lines = back_ref.shape[0] // n_dp
+    per_block = BACK_PARTS * slots
+    members = back_ref.shape[0] // n_dp
+    lines = members * per_block
     line = lax.broadcasted_iota(jnp.int32, (1, lines), 1)
-    expert = line // (PARTS * slots * per_expert)
-    part = (line // slots) % PARTS
+    expert = line // (per_block * per_expert)
+    part = (line // slots) % BACK_PARTS
     slot = line % slots
     ids = ids_ref[...]
     seen = jnp.zeros((1, lines), jnp.int32)
@@ -296,23 +311,22 @@
         named = functools.reduce(lambda a, b: a | b, same)
         chosen = named & (seen == slot)
         seen = seen + named.astype(jnp.int32)
-        for p in range(PARTS - 1):
+        for p in range(BACK_PARTS):
             gather[p * count + t : p * count + t + 1, :] = (chosen & (part == p)).astype(F32)
         for k in range(TOPK):
-            row = (PARTS - 1 + k) * count + t
-            gather[row : row + 1, :] = (chosen & same[k] & (part == PARTS - 1)).astype(F32)
+            row = (BACK_PARTS + k) * count + t
+            gather[row : row + 1, :] = (chosen & same[k] & (part == BACK_PARTS - 1)).astype(F32)
     sums = gather[...].astype(BF16)
     route = jnp.zeros((TOPK * count, 1), F32)
+    tail = rows - back_wide
     for j in range(n_dp):
-        block = dot(sums, back_ref[j * lines : (j + 1) * lines, :], ((1,), (0,)))
-        for p in range(PARTS - 1):
-            width = min(back_wide, rows - p * back_wide)
-            if width > 0:
-                first = j * rows + p * back_wide
-                tokens_ref[:, first : first + width] = block[p * count : (p + 1) * count, :width].astype(BF16)
+        arrived = back_ref[j * members : (j + 1) * members].astype(F32).reshape(lines, back_wide).astype(BF16)
+        block = dot(sums, arrived, ((1,), (0,)))
+        tokens_ref[:, j * rows : j * rows + back_wide] = block[0:count].astype(BF16)
+        tokens_ref[:, j * rows + back_wide : (j + 1) * rows] = block[count : 2 * count, :tail].astype(BF16)
         if j < CORES:
-            terms = block[(PARTS - 1) * count : (PARTS - 1 + TOPK) * count]
-            route = route + terms[:, 0:1] + terms[:, 1:2]
+            terms = block[BACK_PARTS * count :]
+            route = route + terms[:, tail : tail + 1] + terms[:, tail + 1 : tail + 2]
     for k in range(TOPK):
         route_ref[:, k : k + 1] = route[k * count : (k + 1) * count]
 
@@ -346,8 +360,7 @@
     count = sources * slots
     per_block = PARTS * slots
     wide = round_up(rows // 2 + 1, LANES)
-    back_wide = round_up(-(-rows // (PARTS - 1)), LANES)
-    group = math.gcd(sources, 32)
+    back_wide = round_up(rows // BACK_PARTS + 1, LANES)
 
     packed = call(
         functools.partial(pack_kernel, n_dp=n_dp, rows=rows, wide=wide, slots=slots),
@@ -391,10 +404,9 @@
         limit=1 << 20,
     )
 
-    inputs, upstream, factor, *sends = call(
-        functools.partial(send_kernel, rows=rows, wide=wide, slots=slots, half=half),
-        [shape((count, rows), BF16), shape((count, rows), BF16), shape((count, 1), F32)]
-        + [shape((count, 3 * width), BF16)] * chunks,
+    inputs, upstream, factor, send = call(
+        functools.partial(send_kernel, rows=rows, wide=wide, slots=slots, half=half, width=width),
+        [shape((count, rows), BF16), shape((count, rows), BF16), shape((count, 1), F32), shape((count, 3 * half), BF16)],
         got.reshape(sources * per_block, wide),
         gate_other,
         up_other,
@@ -403,7 +415,7 @@
         moved=1 << 20,
     )
     swap = [(i, i ^ 1) for i in range(n_dp)]
-    arrived = [lax.ppermute(send, "dp", swap) for send in sends]
+    arrived = lax.ppermute(send, "dp", swap)
     keeps, pairs, gate_owns, up_owns, others = [], [], [], [], []
     for q in range(chunks):
         keep, gate_own, up_own = call(
@@ -420,10 +432,10 @@
             far=(2, 3, 4),
         )
         pair, low = call(
-            pair_kernel,
+            functools.partial(pair_kernel, q=q),
             [shape((count, 3 * width), F32), shape((count, 3 * width), BF16)],
             keep,
-            arrived[q],
+            arrived,
             moved=1 << 20,
         )
         gate_owns.append(gate_own)
@@ -434,17 +446,19 @@
             perm = [(i, (i + shift * CORES) % n_dp) for i in range(n_dp)]
             passed.append(lax.ppermute(low, "dp", perm))
         others.append(passed)
-    derived, dots, earlier = [], [], []
+    derived, dots, earlier, turned = [], [], [], []
     for q in range(chunks):
         outs = [shape((count, 3 * width), BF16), shape((count, 1), F32)]
         if q < chunks - 1:
-            own, dot_terms, part = call(
+            own, dot_terms, part, *turned = call(
                 functools.partial(derive_back_kernel, half=width),
-                [*outs, shape((count, rows), F32)],
+                [*outs, shape((count, rows), F32), shape((width, rows), BF16), shape((width, rows), BF16)],
                 pairs[q],
                 factor,
                 gate_owns[q],
                 up_owns[q],
+                gate_other,
+                up_other,
                 *others[q],
                 flops=4 * count * rows * width,
                 moved=1 << 20,
@@ -477,23 +491,17 @@
             rows=rows,
             back_wide=back_wide,
             slots=slots,
+            turned=bool(turned),
         ),
-        shape((sources * per_block, back_wide), BF16),
+        shape((sources, BACK_PARTS * slots, back_wide), BF16),
         other,
         part,
-        gate_other,
-        up_other,
+        *(turned or (gate_other, up_other)),
         *dots,
-        scratch=[
-            pltpu.VMEM((count, (PARTS - 1) * back_wide), BF16),
-            pltpu.VMEM((group * per_block, back_wide), BF16),
-        ],
         flops=4 * count * rows * width,
         moved=1 << 20,
     )
-    back = lax.all_to_all(
-        back.reshape(sources, per_block, back_wide), ("dp", "expert"), split_axis=0, concat_axis=0, tiled=True
-    )
+    back = lax.all_to_all(back, ("dp", "expert"), split_axis=0, concat_axis=0, tiled=True)
     grads = call(
         functools.partial(grad_kernel, half=half, width=width),
         [shape((rows, hidden_units), BF16)] * 3,
@@ -510,8 +518,8 @@
         ),
         [shape((token_count, model_width), BF16), shape((token_count, TOPK), F32)],
         expert_ids,
-        back.reshape(sources * per_block, back_wide),
-        scratch=[pltpu.VMEM(((PARTS - 1 + TOPK) * token_count, members * per_block), F32)],
+        back,
+        scratch=[pltpu.VMEM(((BACK_PARTS + TOPK) * token_count, members * BACK_PARTS * slots), F32)],
         moved=1 << 18,
     )
     return (d_tokens, d_route, *grads)

time: 45.9 us -> 45.4 us (0.989)
  transfers between devices with their start and end apart: 8 -> 7, of which waited for: 5 -> 5; matrix products, arithmetic and copies ran while one was open for 0% -> 0% of each run, Pallas kernels for 27% -> 27%
where the time goes in v4:
time: 45.4 us; the launch traced here: 45 us
  Pallas kernels  17 us (37%)
  waiting for transfers between devices  14.3 us (31%)
  starting transfers between devices  12.9 us (28%)
  between operations  0.79 us (2%)
    pallas_call x13, Pallas kernels, call(): pl.pallas_call(kernel, out_shape=outs, in_specs=[pl.BlockSpec(memory_spac...  17 us
    all_to_all x1, starting transfers between devices, local(): lax.all_to_all(packed, ('dp', 'expert'), split_axis=0, concat_axis=0, til...  7.3 us
    all_to_all x1, waiting for transfers between devices, local(): lax.all_to_all(packed, ('dp', 'expert'), split_axis=0, concat_axis=0, til...  6.58 us
    ppermute x2, waiting for transfers between devices, local(): passed.append(lax.ppermute(low, 'dp', perm))  4.65 us
    all_to_all x1, starting transfers between devices, local(): lax.all_to_all(back, ('dp', 'expert'), split_axis=0, concat_axis=0, tiled...  3.06 us
    all_to_all x1, waiting for transfers between devices, local(): lax.all_to_all(back, ('dp', 'expert'), split_axis=0, concat_axis=0, tiled...  2.62 us
    ppermute x2, starting transfers between devices, local(): passed.append(lax.ppermute(low, 'dp', perm))  2.16 us
  transfers between devices with their start and end apart: 7, of which 5 were waited for; matrix products, arithmetic and copies ran while one was open for 0% of the time, Pallas kernels for 27%

profile of v4, /device:TPU:0, one launch (start us, length us, event | category | flops | bytes accessed | tf_op | source)
XLA Modules:
  0.0 45.0 jit_solution(8978457843262378438)
XLA Ops:
  0.6 2.0 %shard_map.110 = bf16[256,384]{1,0:T(8,128)(2,1)} custom-call(s32[4,4]{1,0:T(4,128)} %ids_ref.1, bf16[4,4]{1,0:T(4,128)(2,1)} %refs_1_.4, bf16[4,2880]{1,0:T(4,128)(2,1)} %refs_2_.4, bf16[4,2880]{1,0:T(4,128)(2,1)} %refs_3_.1), custom_call_target="tpu_custom_call" | custom-call | bytes 262144 | tf_op jit(solution)/shard_map/pallas_call | solution.py:336
  2.6 7.3 %all-to-all-start = ((bf16[32,8,384]{2,1,0:T(8,128)(2,1)}), bf16[32,8,384]{2,1,0:T(8,128)(2,1)S(1)}, u32[]{:S(2)}, u32[]{:S(2)}) async-start(bf16[32,8,384]{2,1,0:T(8,128)(2,1)} %bitcast.order_ref), calls=%async_computation | async-start | bytes 393216 | tf_op jit(solution)/shard_map/all_to_all | solution.py:387
  9.9 2.0 %shard_map.111 = (bf16[720,768]{1,0:T(8,128)(2,1)S(1)}, bf16[720,768]{1,0:T(8,128)(2,1)S(1)}, bf16[720,768]{1,0:T(8,128)(2,1)S(1)}) custom-call(bf16[32,8,384]{2,1,0:T(8,128)(2,1)} %bitcast.order_ref, bf16[720,1536]{1,0:T(8,128)(2,1)} %refs_0_.7, bf16[720,1536]{1,0:T(8,128)(2,1)} %refs_1_.7, bf16[720,1536]{1,0:T(8,128)(2,1)} %refs_2_.7), custom_call_target="tpu_custom_call" | custom-call | bytes 3317760 | tf_op jit(solution)/shard_map/pallas_call | solution.py:336
  11.9 6.6 %all-to-all-done = bf16[32,8,384]{2,1,0:T(8,128)(2,1)S(1)} async-done(((bf16[32,8,384]{2,1,0:T(8,128)(2,1)}), bf16[32,8,384]{2,1,0:T(8,128)(2,1)S(1)}, u32[]{:S(2)}, u32[]{:S(2)}) %all-to-all-start) | async-done | bytes 196640 | tf_op jit(solution)/shard_map/all_to_all | solution.py:387
  18.5 0.8 %shard_map.112 = (bf16[64,720]{1,0:T(8,128)(2,1)S(1)}, bf16[64,720]{1,0:T(8,128)(2,1)S(1)}, f32[64,1]{1,0:T(8,128)S(1)}, bf16[64,2304]{1,0:T(8,128)(2,1)S(1)}) custom-call(bf16[256,384]{1,0:T(8,128)(2,1)S(1)} %bitcast.2, bf16[720,768]{1,0:T(8,128)(2,1)S(1)} %get-tuple-element.34.gate_ref.gate_other.refs_0_, ...), custom_call_target="tpu_custom_call" | custom-call | flops 212336640 | bytes 1048576 | tf_op jit(solution)/shard_map/pallas_call | solution.py:336
  19.3 0.0 copy-start
  19.3 0.0 copy-start.2
  19.4 0.2 collective-permute-start
  19.6 1.8 %shard_map.116 = (f32[64,1152]{1,0:T(8,128)S(1)}, bf16[720,384]{1,0:T(8,128)(2,1)S(1)}, bf16[720,384]{1,0:T(8,128)(2,1)S(1)}) custom-call(bf16[64,720]{1,0:T(8,128)(2,1)S(1)} %get-tuple-element.37.inputs_ref, bf16[64,720]{1,0:T(8,128)(2,1)S(1)} %get-tuple-element.38.upstream_ref, bf16[720,1536]{1,0:T(8,128)(2,1)} %refs_0_.7, bf16[720,1536]{1,0:T(8,128)(2,1)} %refs_1_.7, ...), custom_call_target="tpu_custom_call" | custom-call | flops 106168320 | bytes 1658880 | tf_op jit(solution)/shard_map/pallas_call | solution.py:336
  21.4 0.0 collective-permute-done.got_ref
  21.5 1.5 %collective-permute-start.3 = (bf16[64,1152]{1,0:T(8,128)(2,1)S(1)}, bf16[64,1152]{1,0:T(8,128)(2,1)S(1)}, u32[]{:S(2)}, u32[]{:S(2)}) collective-permute-start(bf16[64,1152]{1,0:T(8,128)(2,1)S(1)} %get-tuple-element.51), channel_id=1, source_target_pairs={{0,16},{8,24},{16,0},{24,8},{1,17},{9,25},{17,1},{25,9},{2,18},{10... | collective-permute-start | bytes 442376 | tf_op jit(solution)/shard_map/ppermute | solution.py:447
  23.0 0.0 copy-done
  23.0 0.0 copy-done.2
  23.0 1.8 %shard_map.113 = (f32[64,1152]{1,0:T(8,128)S(1)}, bf16[720,384]{1,0:T(8,128)(2,1)S(1)}, bf16[720,384]{1,0:T(8,128)(2,1)S(1)}) custom-call(bf16[64,720]{1,0:T(8,128)(2,1)S(1)} %get-tuple-element.37.inputs_ref, bf16[64,720]{1,0:T(8,128)(2,1)S(1)} %get-tuple-element.38.upstream_ref, bf16[720,1536]{1,0:T(8,128)(2,1)} %refs_0_.7, bf16[720,1536]{1,0:T(8,128)(2,1)} %refs_1_.7, ...), custom_call_target="tpu_custom_call" | custom-call | flops 106168320 | bytes 1658880 | tf_op jit(solution)/shard_map/pallas_call | solution.py:336
  24.9 0.6 %collective-permute-start.1 = (bf16[64,1152]{1,0:T(8,128)(2,1)S(1)}, bf16[64,1152]{1,0:T(8,128)(2,1)S(1)}, u32[]{:S(2)}, u32[]{:S(2)}) collective-permute-start(bf16[64,1152]{1,0:T(8,128)(2,1)S(1)} %get-tuple-element.43), channel_id=1, source_target_pairs={{0,16},{8,24},{16,0},{24,8},{1,17},{9,25},{17,1},{25,9},{2,18},{10... | collective-permute-start | bytes 442376 | tf_op jit(solution)/shard_map/ppermute | solution.py:447
  25.5 2.4 %collective-permute-done.3.refs_0_ = bf16[64,1152]{1,0:T(8,128)(2,1)S(1)} collective-permute-done((bf16[64,1152]{1,0:T(8,128)(2,1)S(1)}, bf16[64,1152]{1,0:T(8,128)(2,1)S(1)}, u32[]{:S(2)}, u32[]{:S(2)}) %collective-permute-start.3) | collective-permute-done | bytes 147488 | tf_op jit(solution)/shard_map/ppermute | solution.py:447
  27.9 0.6 %shard_map.118 = (bf16[64,1152]{1,0:T(8,128)(2,1)S(1)}, f32[64,1]{1,0:T(8,128)S(1)}, f32[64,720]{1,0:T(8,128)S(1)}, bf16[384,720]{1,0:T(8,128)(2,1)S(1)}, bf16[384,720]{1,0:T(8,128)(2,1)S(1)}) custom-call(f32[64,1152]{1,0:T(8,128)S(1)} %get-tuple-element.48.pair_ref, f32[64,1]{1,0:T(8,128)S(1)} %get-tuple-element.42.factor_ref, ...), custom_call_target="tpu_custom_call" | custom-call | flops 70778880 | bytes 1048576 | tf_op jit(solution)/shard_map/pallas_call | solution.py:336
  28.5 0.1 collective-permute-start.4
  28.5 2.3 %collective-permute-done.1.refs_0_ = bf16[64,1152]{1,0:T(8,128)(2,1)S(1)} collective-permute-done((bf16[64,1152]{1,0:T(8,128)(2,1)S(1)}, bf16[64,1152]{1,0:T(8,128)(2,1)S(1)}, u32[]{:S(2)}, u32[]{:S(2)}) %collective-permute-start.1) | collective-permute-done | bytes 147488 | tf_op jit(solution)/shard_map/ppermute | solution.py:447
  30.8 0.1 shard_map.115
  30.9 0.0 collective-permute-start.2
  31.0 0.0 collective-permute-done.4.refs_3_.refs_1_
  31.0 0.0 copy-start.1
  31.0 0.0 copy-start.3
  31.0 0.8 %shard_map.119.part_ref = f32[64,720]{1,0:T(8,128)S(1)} custom-call(bf16[64,1152]{1,0:T(8,128)(2,1)S(1)} %get-tuple-element.44.own_ref.refs_2_, bf16[720,384]{1,0:T(8,128)(2,1)S(1)} %get-tuple-element.45.gate_own, bf16[720,384]{1,0:T(8,128)(2,1)S(1)} %get-tuple-element.46.up_own, bf16[720,768]{1,0:T(8,128)(2,1)S(1)} %get-tuple-element.34.gate_ref.gate_other.refs_0_, ...), custom_call_target="tpu_custom_call" | custom-call | flops 141557760 | bytes 1048576 | tf_op jit(solution)/shard_map/pallas_call | solution.py:336
  31.9 0.0 copy-start.4
  31.9 0.5 %collective-permute-done.2.other_ref.refs_3_ = bf16[64,1152]{1,0:T(8,128)(2,1)S(1)} collective-permute-done((bf16[64,1152]{1,0:T(8,128)(2,1)S(1)}, bf16[64,1152]{1,0:T(8,128)(2,1)S(1)}, u32[]{:S(2)}, u32[]{:S(2)}) %collective-permute-start.2) | collective-permute-done | bytes 147488 | tf_op jit(solution)/shard_map/ppermute | solution.py:472
  32.3 1.1 %shard_map.120 = bf16[32,4,384]{2,1,0:T(4,128)(2,1)} custom-call(bf16[64,1152]{1,0:T(8,128)(2,1)S(1)} %collective-permute-done.2.other_ref.refs_3_, f32[64,720]{1,0:T(8,128)S(1)} %shard_map.119.part_ref, bf16[384,720]{1,0:T(8,128)(2,1)S(1)} %get-tuple-element.54.gate_ref, bf16[384,720]{1,0:T(8,128)(2,1)S(1)} %get-tuple-element.55.up_ref, ...), custom_call_target="tpu_custom_call" | custom-call | flops 70778880 | bytes 1048576 | tf_op jit(solution)/shard_map/pallas_call | solution.py:336
  33.5 3.1 %all-to-all-start.1 = ((bf16[32,4,384]{2,1,0:T(4,128)(2,1)}), bf16[32,4,384]{2,1,0:T(4,128)(2,1)S(1)}, u32[]{:S(2)}, u32[]{:S(2)}) async-start(bf16[32,4,384]{2,1,0:T(4,128)(2,1)} %shard_map.120), calls=%async_computation.1 | async-start | bytes 196608 | tf_op jit(solution)/shard_map/all_to_all | solution.py:504
  36.5 0.0 copy-done.1
  36.5 0.0 copy-done.3
  36.6 4.9 %shard_map.122 = (bf16[720,1536]{1,0:T(8,128)(2,1)}, bf16[720,1536]{1,0:T(8,128)(2,1)}, bf16[720,1536]{1,0:T(8,128)(2,1)}) custom-call(bf16[64,720]{1,0:T(8,128)(2,1)S(1)} %copy-done.1, bf16[64,720]{1,0:T(8,128)(2,1)S(1)} %copy-done.3, f32[64,1]{1,0:T(8,128)S(1)} %get-tuple-element.42.factor_ref, bf16[64,1152]{1,0:T(8,128)(2,1)S(1)} %get-tuple-element.53.refs_0_, ...), custom_call_target="tpu_custom_call" | custom-call | flops 424673280 | bytes 6635520 | tf_op jit(solution)/shard_map/pallas_call | solution.py:336
  41.5 2.6 %all-to-all-done.1.back_ref = bf16[32,4,384]{2,1,0:T(4,128)(2,1)S(1)} async-done(((bf16[32,4,384]{2,1,0:T(4,128)(2,1)}), bf16[32,4,384]{2,1,0:T(4,128)(2,1)S(1)}, u32[]{:S(2)}, u32[]{:S(2)}) %all-to-all-start.1) | async-done | bytes 98336 | tf_op jit(solution)/shard_map/all_to_all | solution.py:504
  44.1 0.0 copy-done.4
  44.1 0.9 %shard_map.121 = (bf16[4,2880]{1,0:T(4,128)(2,1)}, f32[4,4]{1,0:T(4,128)}) custom-call(s32[4,4]{1,0:T(4,128)S(1)} %copy-done.4, bf16[32,4,384]{2,1,0:T(4,128)(2,1)S(1)} %all-to-all-done.1.back_ref), custom_call_target="tpu_custom_call" | custom-call | bytes 262144 | tf_op jit(solution)/shard_map/pallas_call | solution.py:336
  (2 shorter events, 0.1 us)
Async XLA Ops:
  2.6 15.9 %all-to-all-start = ((bf16[32,8,384]{2,1,0:T(8,128)(2,1)}), bf16[32,8,384]{2,1,0:T(8,128)(2,1)S(1)}, u32[]{:S(2)}, u32[]{:S(2)}) async-start(bf16[32,8,384]{2,1,0:T(8,128)(2,1)} %bitcast.order_ref), calls=%async_computation | async-start | bytes 393216 | tf_op jit(solution)/shard_map/all_to_all | solution.py:387
  19.3 3.7 %copy-start = (bf16[64,720]{1,0:T(8,128)(2,1)}, bf16[64,720]{1,0:T(8,128)(2,1)S(1)}, u32[]{:S(2)}) copy-start(bf16[64,720]{1,0:T(8,128)(2,1)S(1)} %get-tuple-element.37.inputs_ref) | copy-start | bytes 276484
  19.3 3.7 %copy-start.2 = (bf16[64,720]{1,0:T(8,128)(2,1)}, bf16[64,720]{1,0:T(8,128)(2,1)S(1)}, u32[]{:S(2)}) copy-start(bf16[64,720]{1,0:T(8,128)(2,1)S(1)} %get-tuple-element.38.upstream_ref) | copy-start | bytes 276484
  19.4 2.1 %collective-permute-start = (bf16[64,2304]{1,0:T(8,128)(2,1)S(1)}, bf16[64,2304]{1,0:T(8,128)(2,1)S(1)}, u32[]{:S(2)}, u32[]{:S(2)}) collective-permute-start(bf16[64,2304]{1,0:T(8,128)(2,1)S(1)} %get-tuple-element.40), channel_id=1, source_target_pairs={{0,8},{8,0},{16,24},{24,16},{1,9},{9,1},{17,25},{25,17},{2,10},{10... | collective-permute-start | bytes 884744 | tf_op jit(solution)/shard_map/ppermute | solution.py:418
  21.5 6.4 %collective-permute-start.3 = (bf16[64,1152]{1,0:T(8,128)(2,1)S(1)}, bf16[64,1152]{1,0:T(8,128)(2,1)S(1)}, u32[]{:S(2)}, u32[]{:S(2)}) collective-permute-start(bf16[64,1152]{1,0:T(8,128)(2,1)S(1)} %get-tuple-element.51), channel_id=1, source_target_pairs={{0,16},{8,24},{16,0},{24,8},{1,17},{9,25},{17,1},{25,9},{2,18},{10... | collective-permute-start | bytes 442376 | tf_op jit(solution)/shard_map/ppermute | solution.py:447
  24.9 5.9 %collective-permute-start.1 = (bf16[64,1152]{1,0:T(8,128)(2,1)S(1)}, bf16[64,1152]{1,0:T(8,128)(2,1)S(1)}, u32[]{:S(2)}, u32[]{:S(2)}) collective-permute-start(bf16[64,1152]{1,0:T(8,128)(2,1)S(1)} %get-tuple-element.43), channel_id=1, source_target_pairs={{0,16},{8,24},{16,0},{24,8},{1,17},{9,25},{17,1},{25,9},{2,18},{10... | collective-permute-start | bytes 442376 | tf_op jit(solution)/shard_map/ppermute | solution.py:447
  28.5 2.5 %collective-permute-start.4 = (bf16[64,1152]{1,0:T(8,128)(2,1)S(1)}, bf16[64,1152]{1,0:T(8,128)(2,1)S(1)}, u32[]{:S(2)}, u32[]{:S(2)}) collective-permute-start(bf16[64,1152]{1,0:T(8,128)(2,1)S(1)} %get-tuple-element.53.refs_0_), channel_id=1, source_target_pairs={{0,8},{8,0},{16,24},{24,16},{1,9},{9,1},{17,25},{25,17},{2,10},{10... | collective-permute-start | bytes 442376 | tf_op jit(solution)/shard_map/ppermute | solution.py:466
  30.9 1.4 %collective-permute-start.2 = (bf16[64,1152]{1,0:T(8,128)(2,1)S(1)}, bf16[64,1152]{1,0:T(8,128)(2,1)S(1)}, u32[]{:S(2)}, u32[]{:S(2)}) collective-permute-start(bf16[64,1152]{1,0:T(8,128)(2,1)S(1)} %get-tuple-element.44.own_ref.refs_2_), channel_id=1, source_target_pairs={{0,8},{8,0},{16,24},{24,16},{1,9},{9,1},{17,25},{25,17},{2,10},{10... | collective-permute-start | bytes 442376 | tf_op jit(solution)/shard_map/ppermute | solution.py:472
  31.0 5.5 %copy-start.1 = (bf16[64,720]{1,0:T(8,128)(2,1)S(1)}, bf16[64,720]{1,0:T(8,128)(2,1)}, u32[]{:S(2)}) copy-start(bf16[64,720]{1,0:T(8,128)(2,1)} %copy-done) | copy-start | bytes 276484
  31.0 5.5 %copy-start.3 = (bf16[64,720]{1,0:T(8,128)(2,1)S(1)}, bf16[64,720]{1,0:T(8,128)(2,1)}, u32[]{:S(2)}) copy-start(bf16[64,720]{1,0:T(8,128)(2,1)} %copy-done.2) | copy-start | bytes 276484
  31.9 12.2 %copy-start.4 = (s32[4,4]{1,0:T(4,128)S(1)}, s32[4,4]{1,0:T(4,128)}, u32[]{:S(2)}) copy-start(s32[4,4]{1,0:T(4,128)} %ids_ref.1) | copy-start | bytes 196
  33.5 10.6 %all-to-all-start.1 = ((bf16[32,4,384]{2,1,0:T(4,128)(2,1)}), bf16[32,4,384]{2,1,0:T(4,128)(2,1)S(1)}, u32[]{:S(2)}, u32[]{:S(2)}) async-start(bf16[32,4,384]{2,1,0:T(4,128)(2,1)} %shard_map.120), calls=%async_computation.1 | async-start | bytes 196608 | tf_op jit(solution)/shard_map/all_to_all | solution.py:504

commit v5 on v4

--- a/solution.py
+++ b/solution.py
@@ -54,49 +54,50 @@
 
 
 def pack_kernel(*refs, n_dp, rows, wide, slots):
-    far, out_ref, near, source, sems = refs[:4], refs[4], refs[5:9], refs[9], refs[10]
+    far, out_ref, near, (source, spread, sems) = refs[:4], refs[4], refs[5:9], refs[9:]
     copies = [pltpu.make_async_copy(far[i], near[i], sems.at[i]) for i in range(4)]
     for copy in copies:
         copy.start()
     ids_ref, weights_ref, tokens_ref, grads_ref = near
     count = tokens_ref.shape[0]
+    taken = PARTS * count
     lines = EXPERTS_F * PARTS * slots
-    line = lax.broadcasted_iota(jnp.int32, (lines, 1), 0)
+    line = lax.broadcasted_iota(jnp.int32, (1, lines), 1)
     expert = line // (PARTS * slots)
     part = (line // slots) % PARTS
     slot = line % slots
-    column = lax.broadcasted_iota(jnp.int32, (lines, PARTS * count), 1)
-    source[...] = jnp.zeros_like(source)
+    single = lax.broadcasted_iota(jnp.int32, source.shape[1:], 0) == taken
+    single = single & (lax.broadcasted_iota(jnp.int32, source.shape[1:], 1) == rows - wide)
+    for j in range(n_dp):
+        source[j] = single.astype(F32)
+    spread[...] = jnp.zeros_like(spread)
     for copy in copies:
         copy.wait()
     ids = ids_ref[...]
     route = weights_ref[...].astype(F32)
-    seen = jnp.zeros((lines, 1), jnp.int32)
-    factor = jnp.zeros((lines, 1), F32)
-    spread = jnp.zeros((lines, PARTS * count), F32)
+    seen = jnp.zeros((1, lines), jnp.int32)
+    factor = jnp.zeros((1, lines), F32)
     for t in range(count):
-        named = jnp.zeros((lines, 1), jnp.int32)
-        value = jnp.zeros((lines, 1), F32)
+        same = [ids[t : t + 1, k : k + 1] == expert for k in range(TOPK)]
+        named = functools.reduce(lambda a, b: a | b, same)
+        chosen = named & (seen == slot)
+        seen = seen + named.astype(jnp.int32)
         for k in range(TOPK):
-            same = ids[t : t + 1, k : k + 1] == expert
-            named = named + same.astype(jnp.int32)
-            value = value + jnp.where(same, route[t : t + 1, k : k + 1], 0.0)
-        chosen = (named > 0) & (seen == slot)
-        seen = seen + (named > 0).astype(jnp.int32)
-        factor = factor + jnp.where(chosen, value, 0.0)
-        spread = spread + jnp.where(chosen & (column == part * count + t), 1.0, 0.0)
-    spread = spread.astype(BF16)
-    lane = lax.broadcasted_iota(jnp.int32, (lines, wide), 1)
-    mark = (lane == rows - wide) & (part % 2 == 1)
+            factor = factor + jnp.where(chosen & same[k], route[t : t + 1, k : k + 1], 0.0)
+        for p in range(PARTS):
+            spread[p * count + t : p * count + t + 1, :] = (chosen & (part == p)).astype(F32)
+    spread[taken : taken + 1, :] = jnp.where(part % 2 == 1, factor, 0.0)
+    move = spread[...].astype(BF16)
     for j in range(n_dp):
         for which, ref in enumerate((tokens_ref, grads_ref)):
             first = 2 * which * count
-            source[first : first + count, :] = ref[:, j * rows : j * rows + wide].astype(F32)
-            source[first + count : first + 2 * count, 0 : rows - wide] = ref[
+            source[j, first : first + count, :] = ref[:, j * rows : j * rows + wide].astype(F32)
+            source[j, first + count : first + 2 * count, 0 : rows - wide] = ref[
                 :, j * rows + wide : (j + 1) * rows
             ].astype(F32)
-        block = dot(spread, source[...].astype(BF16), ((1,), (0,)))
-        out_ref[j * lines : (j + 1) * lines, :] = jnp.where(mark, factor, block).astype(BF16)
+    for j in range(n_dp):
+        block = dot(move, source[j].astype(BF16), ((0,), (0,)))
+        out_ref[j * lines : (j + 1) * lines, :] = block.astype(BF16)
 
 
 def stage_kernel(order_ref, *refs, half):
@@ -220,8 +221,20 @@
     back_product(my_core(), half, half, 0, own_ref, gate_ref, up_ref, write)
 
 
-def back_part_kernel(own_ref, gate_own, up_own, *refs, half, width):
-    out_ref = refs[-1]
+def back_part_kernel(own_ref, gate_own, up_own, *refs, half, width, chunks, tail, slots):
+    dots_refs, (out_ref, move_ref, ending_ref) = refs[:chunks], refs[-3:]
+    refs = (*refs[chunks:-3], out_ref)
+    per_block = BACK_PARTS * slots
+    lines = move_ref.shape[0]
+    group = lines // per_block
+    column = lax.broadcasted_iota(jnp.int32, (1, lines), 1)
+    target = (column % group) * per_block + column // group
+    move_ref[...] = (lax.broadcasted_iota(jnp.int32, (lines, lines), 0) == target).astype(F32).astype(BF16)
+    dots = functools.reduce(lambda x, y: x + y, [ref[...] for ref in dots_refs])
+    high = dots.astype(BF16).astype(F32)
+    lane = lax.broadcasted_iota(jnp.int32, ending_ref.shape, 1)
+    ending = jnp.where(lane == tail, high, jnp.where(lane == tail + 1, dots - high, 0.0))
+    ending_ref[...] = ending.astype(BF16)
 
     def write(value):
         out_ref[...] = value
@@ -238,20 +251,11 @@
             back_product(1 - my_core(), half, width, q * width, earlier[2 * q + 1], gate_other, up_other, add)
 
 
-def back_kernel(other_ref, part_ref, gate_ref, up_ref, *refs, half, width, first, rows, back_wide, slots, turned):
-    dots_refs, out_ref = refs[:-1], refs[-1]
-    per_block = BACK_PARTS * slots
-    sources = out_ref.shape[0]
-    group = math.gcd(sources, 32)
-    lines = group * per_block
-    column = lax.broadcasted_iota(jnp.int32, (1, lines), 1)
-    target = (column % group) * per_block + column // group
-    move = (lax.broadcasted_iota(jnp.int32, (lines, lines), 0) == target).astype(F32).astype(BF16)
-    dots = functools.reduce(lambda x, y: x + y, [ref[...] for ref in dots_refs])
-    high = dots.astype(BF16).astype(F32)
-    tail = rows - back_wide
-    lane = lax.broadcasted_iota(jnp.int32, (dots.shape[0], back_wide - tail), 1)
-    ending = jnp.where(lane == 0, high, jnp.where(lane == 1, dots - high, 0.0))
+def back_kernel(
+    other_ref, part_ref, move_ref, ending_ref, gate_ref, up_ref, out_ref, *, half, width, first, rows, slots, turned
+):
+    sources, per_block, back_wide = out_ref.shape
+    group = move_ref.shape[0] // per_block
 
     def body(base):
         columns = pl.ds(base + first, width)
@@ -265,22 +269,23 @@
                 else:
                     value = value + dot(left, weight_ref[lower:upper, columns], ((1,), (1,)))
             blocks.append(value)
-        blocks[1] = jnp.concatenate([blocks[1], ending], axis=1)
         blocks = [block.astype(BF16) for block in blocks]
+        blocks[1] = jnp.concatenate([blocks[1], ending_ref[:, rows - back_wide :]], axis=1)
         for g in range(sources // group):
             stacked = [
                 block[s * sources + g * group : s * sources + (g + 1) * group] for block in blocks for s in range(slots)
             ]
             if sources == group:
                 stacked = blocks
-            moved = dot(move, jnp.concatenate(stacked, axis=0), ((1,), (0,)))
+            moved = dot(move_ref[...], jnp.concatenate(stacked, axis=0), ((1,), (0,)))
             out_ref[g * group : (g + 1) * group] = moved.reshape(group, per_block, back_wide).astype(BF16)
 
     at_half(1 - my_core(), half, half if turned else gate_ref.shape[1], body)
 
 
-def grad_kernel(inputs_ref, upstream_ref, factor_ref, *refs, half, width):
-    derived, outs = refs[:-3], refs[-3:]
+def grad_kernel(ids_ref, inputs_ref, upstream_ref, factor_ref, *refs, half, width, slots, per_expert):
+    derived, outs, (sums_ref, gather) = refs[:-5], refs[-5:-2], refs[-2:]
+    select_rows(ids_ref, gather, sums_ref, slots, per_expert)
     core = my_core()
     scaled = (factor_ref[...] * upstream_ref[...].astype(F32)).astype(BF16)
     lefts = (inputs_ref[...], inputs_ref[...], scaled)
@@ -295,13 +300,11 @@
         at_half(core if n % CORES == 0 else 1 - core, half, outs[0].shape[1], body)
 
 
-def combine_kernel(ids_ref, back_ref, tokens_ref, route_ref, gather, *, n_dp, rows, back_wide, slots, per_expert):
-    count = tokens_ref.shape[0]
-    per_block = BACK_PARTS * slots
-    members = back_ref.shape[0] // n_dp
-    lines = members * per_block
+def select_rows(ids_ref, gather, sums_ref, slots, per_expert):
+    count = ids_ref.shape[0]
+    lines = gather.shape[1]
     line = lax.broadcasted_iota(jnp.int32, (1, lines), 1)
-    expert = line // (per_block * per_expert)
+    expert = line // (BACK_PARTS * slots * per_expert)
     part = (line // slots) % BACK_PARTS
     slot = line % slots
     ids = ids_ref[...]
@@ -316,7 +319,14 @@
         for k in range(TOPK):
             row = (BACK_PARTS + k) * count + t
             gather[row : row + 1, :] = (chosen & same[k] & (part == BACK_PARTS - 1)).astype(F32)
-    sums = gather[...].astype(BF16)
+    sums_ref[...] = gather[...].astype(BF16)
+
+
+def combine_kernel(sums_ref, back_ref, tokens_ref, route_ref, *, n_dp, rows, back_wide):
+    count = tokens_ref.shape[0]
+    members = back_ref.shape[0] // n_dp
+    lines = sums_ref.shape[1]
+    sums = sums_ref[...]
     route = jnp.zeros((TOPK * count, 1), F32)
     tail = rows - back_wide
     for j in range(n_dp):
@@ -374,7 +384,8 @@
             pltpu.VMEM(route_weights.shape, BF16),
             pltpu.VMEM(tokens.shape, BF16),
             pltpu.VMEM(cotangent.shape, BF16),
-            pltpu.VMEM((PARTS * token_count, wide), F32),
+            pltpu.VMEM((n_dp, round_up(PARTS * token_count + 1, 8), wide), F32),
+            pltpu.VMEM((round_up(PARTS * token_count + 1, 8), EXPERTS_F * per_block), F32),
             pltpu.SemaphoreType.DMA((4,)),
         ],
         moved=1 << 18,
@@ -472,12 +483,16 @@
             other = lax.ppermute(own, "dp", swap)
         derived += [own, other]
         dots.append(dot_terms)
-    part = call(
-        functools.partial(back_part_kernel, half=half, width=width),
-        shape((count, rows), F32),
+    lines = math.gcd(sources, 32) * BACK_PARTS * slots
+    part, move, ending = call(
+        functools.partial(
+            back_part_kernel, half=half, width=width, chunks=chunks, tail=rows - back_wide, slots=slots
+        ),
+        [shape((count, rows), F32), shape((lines, lines), BF16), shape((count, back_wide), BF16)],
         own,
         gate_owns[-1],
         up_owns[-1],
+        *dots,
         *((gate_other, up_other, *earlier) if earlier else ()),
         flops=4 * count * rows * half,
         moved=1 << 20,
@@ -489,37 +504,37 @@
             width=width,
             first=half - width,
             rows=rows,
-            back_wide=back_wide,
             slots=slots,
             turned=bool(turned),
         ),
         shape((sources, BACK_PARTS * slots, back_wide), BF16),
         other,
         part,
+        move,
+        ending,
         *(turned or (gate_other, up_other)),
-        *dots,
         flops=4 * count * rows * width,
         moved=1 << 20,
     )
     back = lax.all_to_all(back, ("dp", "expert"), split_axis=0, concat_axis=0, tiled=True)
-    grads = call(
-        functools.partial(grad_kernel, half=half, width=width),
-        [shape((rows, hidden_units), BF16)] * 3,
+    select = ((BACK_PARTS + TOPK) * token_count, members * BACK_PARTS * slots)
+    *grads, sums = call(
+        functools.partial(grad_kernel, half=half, width=width, slots=slots, per_expert=per_expert),
+        [shape((rows, hidden_units), BF16)] * 3 + [shape(select, BF16)],
+        expert_ids,
         inputs,
         upstream,
         factor,
         *derived,
+        scratch=[pltpu.VMEM(select, F32)],
         flops=12 * count * rows * half,
         moved=6 * rows * hidden_units,
     )
     d_tokens, d_route = call(
-        functools.partial(
-            combine_kernel, n_dp=n_dp, rows=rows, back_wide=back_wide, slots=slots, per_expert=per_expert
-        ),
+        functools.partial(combine_kernel, n_dp=n_dp, rows=rows, back_wide=back_wide),
         [shape((token_count, model_width), BF16), shape((token_count, TOPK), F32)],
-        expert_ids,
+        sums,
         back,
-        scratch=[pltpu.VMEM(((BACK_PARTS + TOPK) * token_count, members * BACK_PARTS * slots), F32)],
         moved=1 << 18,
     )
     return (d_tokens, d_route, *grads)

time: 45.4 us -> 45.2 us (level)
  no operation moved by 1% of the time
where the time goes in v5:
time: 45.2 us; the launch traced here: 44.8 us
  Pallas kernels  16.8 us (37%)
  waiting for transfers between devices  14.3 us (32%)
  starting transfers between devices  12.9 us (29%)
  between operations  0.8 us (2%)
    pallas_call x13, Pallas kernels, call(): pl.pallas_call(kernel, out_shape=outs, in_specs=[pl.BlockSpec(memory_spac...  16.8 us
    all_to_all x1, starting transfers between devices, local(): lax.all_to_all(packed, ('dp', 'expert'), split_axis=0, concat_axis=0, til...  7.3 us
    all_to_all x1, waiting for transfers between devices, local(): lax.all_to_all(packed, ('dp', 'expert'), split_axis=0, concat_axis=0, til...  6.58 us
    ppermute x2, waiting for transfers between devices, local(): passed.append(lax.ppermute(low, 'dp', perm))  4.64 us
    all_to_all x1, starting transfers between devices, local(): lax.all_to_all(back, ('dp', 'expert'), split_axis=0, concat_axis=0, tiled...  3.06 us
    all_to_all x1, waiting for transfers between devices, local(): lax.all_to_all(back, ('dp', 'expert'), split_axis=0, concat_axis=0, tiled...  2.59 us
    ppermute x2, starting transfers between devices, local(): passed.append(lax.ppermute(low, 'dp', perm))  2.16 us
  transfers between devices with their start and end apart: 7, of which 5 were waited for; matrix products, arithmetic and copies ran while one was open for 0% of the time, Pallas kernels for 27%

profile of v5, /device:TPU:0, one launch (start us, length us, event | category | flops | bytes accessed | tf_op | source)
XLA Modules:
  0.0 44.8 jit_solution(2639032723426371221)
XLA Ops:
  0.6 1.8 %shard_map.110 = bf16[256,384]{1,0:T(8,128)(2,1)} custom-call(s32[4,4]{1,0:T(4,128)} %ids_ref.1, bf16[4,4]{1,0:T(4,128)(2,1)} %refs_1_.4, bf16[4,2880]{1,0:T(4,128)(2,1)} %refs_2_.4, bf16[4,2880]{1,0:T(4,128)(2,1)} %refs_3_.1), custom_call_target="tpu_custom_call" | custom-call | bytes 262144 | tf_op jit(solution)/shard_map/pallas_call | solution.py:346
  2.5 7.3 %all-to-all-start = ((bf16[32,8,384]{2,1,0:T(8,128)(2,1)}), bf16[32,8,384]{2,1,0:T(8,128)(2,1)S(1)}, u32[]{:S(2)}, u32[]{:S(2)}) async-start(bf16[32,8,384]{2,1,0:T(8,128)(2,1)} %bitcast.order_ref), calls=%async_computation | async-start | bytes 393216 | tf_op jit(solution)/shard_map/all_to_all | solution.py:398
  9.8 2.0 %shard_map.111 = (bf16[720,768]{1,0:T(8,128)(2,1)S(1)}, bf16[720,768]{1,0:T(8,128)(2,1)S(1)}, bf16[720,768]{1,0:T(8,128)(2,1)S(1)}) custom-call(bf16[32,8,384]{2,1,0:T(8,128)(2,1)} %bitcast.order_ref, bf16[720,1536]{1,0:T(8,128)(2,1)} %refs_0_.7, bf16[720,1536]{1,0:T(8,128)(2,1)} %refs_1_.7, bf16[720,1536]{1,0:T(8,128)(2,1)} %refs_2_.7), custom_call_target="tpu_custom_call" | custom-call | bytes 3317760 | tf_op jit(solution)/shard_map/pallas_call | solution.py:346
  11.7 6.6 %all-to-all-done = bf16[32,8,384]{2,1,0:T(8,128)(2,1)S(1)} async-done(((bf16[32,8,384]{2,1,0:T(8,128)(2,1)}), bf16[32,8,384]{2,1,0:T(8,128)(2,1)S(1)}, u32[]{:S(2)}, u32[]{:S(2)}) %all-to-all-start) | async-done | bytes 196640 | tf_op jit(solution)/shard_map/all_to_all | solution.py:398
  18.3 0.8 %shard_map.112 = (bf16[64,720]{1,0:T(8,128)(2,1)S(1)}, bf16[64,720]{1,0:T(8,128)(2,1)S(1)}, f32[64,1]{1,0:T(8,128)S(1)}, bf16[64,2304]{1,0:T(8,128)(2,1)S(1)}) custom-call(bf16[256,384]{1,0:T(8,128)(2,1)S(1)} %bitcast.2, bf16[720,768]{1,0:T(8,128)(2,1)S(1)} %get-tuple-element.38.gate_ref.gate_other.refs_2_, ...), custom_call_target="tpu_custom_call" | custom-call | flops 212336640 | bytes 1048576 | tf_op jit(solution)/shard_map/pallas_call | solution.py:346
  19.2 0.0 copy-start
  19.2 0.0 copy-start.2
  19.2 0.2 collective-permute-start
  19.4 1.8 %shard_map.113 = (f32[64,1152]{1,0:T(8,128)S(1)}, bf16[720,384]{1,0:T(8,128)(2,1)S(1)}, bf16[720,384]{1,0:T(8,128)(2,1)S(1)}) custom-call(bf16[64,720]{1,0:T(8,128)(2,1)S(1)} %get-tuple-element.41.inputs_ref, bf16[64,720]{1,0:T(8,128)(2,1)S(1)} %get-tuple-element.42.upstream_ref, bf16[720,1536]{1,0:T(8,128)(2,1)} %refs_0_.7, bf16[720,1536]{1,0:T(8,128)(2,1)} %refs_1_.7, ...), custom_call_target="tpu_custom_call" | custom-call | flops 106168320 | bytes 1658880 | tf_op jit(solution)/shard_map/pallas_call | solution.py:346
  21.2 0.0 collective-permute-done.got_ref
  21.3 0.1 shard_map.114
  21.3 1.5 %collective-permute-start.1 = (bf16[64,1152]{1,0:T(8,128)(2,1)S(1)}, bf16[64,1152]{1,0:T(8,128)(2,1)S(1)}, u32[]{:S(2)}, u32[]{:S(2)}) collective-permute-start(bf16[64,1152]{1,0:T(8,128)(2,1)S(1)} %get-tuple-element.49), channel_id=1, source_target_pairs={{0,16},{8,24},{16,0},{24,8},{1,17},{9,25},{17,1},{25,9},{2,18},{10... | collective-permute-start | bytes 442376 | tf_op jit(solution)/shard_map/ppermute | solution.py:458
  22.9 0.0 copy-done
  22.9 0.0 copy-done.2
  22.9 1.8 %shard_map.116 = (f32[64,1152]{1,0:T(8,128)S(1)}, bf16[720,384]{1,0:T(8,128)(2,1)S(1)}, bf16[720,384]{1,0:T(8,128)(2,1)S(1)}) custom-call(bf16[64,720]{1,0:T(8,128)(2,1)S(1)} %get-tuple-element.41.inputs_ref, bf16[64,720]{1,0:T(8,128)(2,1)S(1)} %get-tuple-element.42.upstream_ref, bf16[720,1536]{1,0:T(8,128)(2,1)} %refs_0_.7, bf16[720,1536]{1,0:T(8,128)(2,1)} %refs_1_.7, ...), custom_call_target="tpu_custom_call" | custom-call | flops 106168320 | bytes 1658880 | tf_op jit(solution)/shard_map/pallas_call | solution.py:346
  24.7 0.1 shard_map.117
  24.7 0.6 %collective-permute-start.3 = (bf16[64,1152]{1,0:T(8,128)(2,1)S(1)}, bf16[64,1152]{1,0:T(8,128)(2,1)S(1)}, u32[]{:S(2)}, u32[]{:S(2)}) collective-permute-start(bf16[64,1152]{1,0:T(8,128)(2,1)S(1)} %get-tuple-element.53), channel_id=1, source_target_pairs={{0,16},{8,24},{16,0},{24,8},{1,17},{9,25},{17,1},{25,9},{2,18},{10... | collective-permute-start | bytes 442376 | tf_op jit(solution)/shard_map/ppermute | solution.py:458
  25.4 2.4 %collective-permute-done.1.refs_0_ = bf16[64,1152]{1,0:T(8,128)(2,1)S(1)} collective-permute-done((bf16[64,1152]{1,0:T(8,128)(2,1)S(1)}, bf16[64,1152]{1,0:T(8,128)(2,1)S(1)}, u32[]{:S(2)}, u32[]{:S(2)}) %collective-permute-start.1) | collective-permute-done | bytes 147488 | tf_op jit(solution)/shard_map/ppermute | solution.py:458
  27.7 0.6 %shard_map.115 = (bf16[64,1152]{1,0:T(8,128)(2,1)S(1)}, f32[64,1]{1,0:T(8,128)S(1)}, f32[64,720]{1,0:T(8,128)S(1)}, bf16[384,720]{1,0:T(8,128)(2,1)S(1)}, bf16[384,720]{1,0:T(8,128)(2,1)S(1)}) custom-call(f32[64,1152]{1,0:T(8,128)S(1)} %get-tuple-element.46.pair_ref, f32[64,1]{1,0:T(8,128)S(1)} %get-tuple-element.43.factor_ref, ...), custom_call_target="tpu_custom_call" | custom-call | flops 70778880 | bytes 1048576 | tf_op jit(solution)/shard_map/pallas_call | solution.py:346
  28.3 0.1 collective-permute-start.2
  28.4 2.3 %collective-permute-done.3.refs_0_ = bf16[64,1152]{1,0:T(8,128)(2,1)S(1)} collective-permute-done((bf16[64,1152]{1,0:T(8,128)(2,1)S(1)}, bf16[64,1152]{1,0:T(8,128)(2,1)S(1)}, u32[]{:S(2)}, u32[]{:S(2)}) %collective-permute-start.3) | collective-permute-done | bytes 147488 | tf_op jit(solution)/shard_map/ppermute | solution.py:458
  30.6 0.1 shard_map.118
  30.8 0.0 collective-permute-start.4
  30.8 0.0 collective-permute-done.2.refs_1_.refs_5_
  30.8 0.0 copy-start.1
  30.9 0.0 copy-start.3
  30.9 0.0 copy-start.4
  30.9 0.8 %shard_map.120 = (f32[64,720]{1,0:T(8,128)S(1)}, bf16[128,128]{1,0:T(8,128)(2,1)S(1)}, bf16[64,384]{1,0:T(8,128)(2,1)S(1)}) custom-call(bf16[64,1152]{1,0:T(8,128)(2,1)S(1)} %get-tuple-element.54.refs_2_.own_ref, bf16[720,384]{1,0:T(8,128)(2,1)S(1)} %get-tuple-element.56.gate_own, bf16[720,384]{1,0:T(8,128)(2,1)S(1)} %get-tuple-element.57.up_own, ...), custom_call_target="tpu_custom_call" | custom-call | flops 141557760 | bytes 1048576 | tf_op jit(solution)/shard_map/pallas_call | solution.py:346
  31.7 0.5 %collective-permute-done.4.refs_3_.other_ref = bf16[64,1152]{1,0:T(8,128)(2,1)S(1)} collective-permute-done((bf16[64,1152]{1,0:T(8,128)(2,1)S(1)}, bf16[64,1152]{1,0:T(8,128)(2,1)S(1)}, u32[]{:S(2)}, u32[]{:S(2)}) %collective-permute-start.4) | collective-permute-done | bytes 147488 | tf_op jit(solution)/shard_map/ppermute | solution.py:483
  32.2 1.1 %shard_map.121 = bf16[32,4,384]{2,1,0:T(4,128)(2,1)} custom-call(bf16[64,1152]{1,0:T(8,128)(2,1)S(1)} %collective-permute-done.4.refs_3_.other_ref, f32[64,720]{1,0:T(8,128)S(1)} %get-tuple-element.61.part_ref, bf16[128,128]{1,0:T(8,128)(2,1)S(1)} %get-tuple-element.62.move_ref, bf16[64,384]{1,0:T(8,128)(2,1)S(1)} %get-tuple-element.63.ending_ref, ...), custom_call_target="tpu_custom_call" | custom-call | flops 70778880 | bytes 1048576 | tf_op jit(solution)/shard_map/pallas_call | solution.py:346
  33.3 3.1 %all-to-all-start.1 = ((bf16[32,4,384]{2,1,0:T(4,128)(2,1)}), bf16[32,4,384]{2,1,0:T(4,128)(2,1)S(1)}, u32[]{:S(2)}, u32[]{:S(2)}) async-start(bf16[32,4,384]{2,1,0:T(4,128)(2,1)} %shard_map.121), calls=%async_computation.1 | async-start | bytes 196608 | tf_op jit(solution)/shard_map/all_to_all | solution.py:519
  36.4 0.0 copy-done.1
  36.4 0.0 copy-done.3
  36.4 0.0 copy-done.4
  36.4 4.9 %shard_map.119 = (bf16[720,1536]{1,0:T(8,128)(2,1)}, bf16[720,1536]{1,0:T(8,128)(2,1)}, bf16[720,1536]{1,0:T(8,128)(2,1)}, bf16[24,32]{1,0:T(8,128)(2,1)S(1)}) custom-call(s32[4,4]{1,0:T(4,128)S(1)} %copy-done.4, bf16[64,720]{1,0:T(8,128)(2,1)S(1)} %copy-done.1, bf16[64,720]{1,0:T(8,128)(2,1)S(1)} %copy-done.3, f32[64,1]{1,0:T(8,128)S(1)} %get-tuple-element.43.factor_ref, ...), custom_call_target="tpu_custom_call" | custom-call | flops 424673280 | bytes 6635520 | tf_op jit(solution)/shard_map/pallas_call | solution.py:346
  41.4 2.6 %all-to-all-done.1.back_ref = bf16[32,4,384]{2,1,0:T(4,128)(2,1)S(1)} async-done(((bf16[32,4,384]{2,1,0:T(4,128)(2,1)}), bf16[32,4,384]{2,1,0:T(4,128)(2,1)S(1)}, u32[]{:S(2)}, u32[]{:S(2)}) %all-to-all-start.1) | async-done | bytes 98336 | tf_op jit(solution)/shard_map/all_to_all | solution.py:519
  44.0 0.9 %shard_map.122 = (bf16[4,2880]{1,0:T(4,128)(2,1)}, f32[4,4]{1,0:T(4,128)}) custom-call(bf16[24,32]{1,0:T(8,128)(2,1)S(1)} %get-tuple-element.55.sums_ref, bf16[32,4,384]{2,1,0:T(4,128)(2,1)S(1)} %all-to-all-done.1.back_ref), custom_call_target="tpu_custom_call" | custom-call | bytes 262144 | tf_op jit(solution)/shard_map/pallas_call | solution.py:346
Async XLA Ops:
  2.5 15.9 %all-to-all-start = ((bf16[32,8,384]{2,1,0:T(8,128)(2,1)}), bf16[32,8,384]{2,1,0:T(8,128)(2,1)S(1)}, u32[]{:S(2)}, u32[]{:S(2)}) async-start(bf16[32,8,384]{2,1,0:T(8,128)(2,1)} %bitcast.order_ref), calls=%async_computation | async-start | bytes 393216 | tf_op jit(solution)/shard_map/all_to_all | solution.py:398
  19.2 3.7 %copy-start = (bf16[64,720]{1,0:T(8,128)(2,1)}, bf16[64,720]{1,0:T(8,128)(2,1)S(1)}, u32[]{:S(2)}) copy-start(bf16[64,720]{1,0:T(8,128)(2,1)S(1)} %get-tuple-element.41.inputs_ref) | copy-start | bytes 276484
  19.2 3.7 %copy-start.2 = (bf16[64,720]{1,0:T(8,128)(2,1)}, bf16[64,720]{1,0:T(8,128)(2,1)S(1)}, u32[]{:S(2)}) copy-start(bf16[64,720]{1,0:T(8,128)(2,1)S(1)} %get-tuple-element.42.upstream_ref) | copy-start | bytes 276484
  19.2 2.1 %collective-permute-start = (bf16[64,2304]{1,0:T(8,128)(2,1)S(1)}, bf16[64,2304]{1,0:T(8,128)(2,1)S(1)}, u32[]{:S(2)}, u32[]{:S(2)}) collective-permute-start(bf16[64,2304]{1,0:T(8,128)(2,1)S(1)} %get-tuple-element.45), channel_id=1, source_target_pairs={{0,8},{8,0},{16,24},{24,16},{1,9},{9,1},{17,25},{25,17},{2,10},{10... | collective-permute-start | bytes 884744 | tf_op jit(solution)/shard_map/ppermute | solution.py:429
  21.3 6.4 %collective-permute-start.1 = (bf16[64,1152]{1,0:T(8,128)(2,1)S(1)}, bf16[64,1152]{1,0:T(8,128)(2,1)S(1)}, u32[]{:S(2)}, u32[]{:S(2)}) collective-permute-start(bf16[64,1152]{1,0:T(8,128)(2,1)S(1)} %get-tuple-element.49), channel_id=1, source_target_pairs={{0,16},{8,24},{16,0},{24,8},{1,17},{9,25},{17,1},{25,9},{2,18},{10... | collective-permute-start | bytes 442376 | tf_op jit(solution)/shard_map/ppermute | solution.py:458
  24.7 5.9 %collective-permute-start.3 = (bf16[64,1152]{1,0:T(8,128)(2,1)S(1)}, bf16[64,1152]{1,0:T(8,128)(2,1)S(1)}, u32[]{:S(2)}, u32[]{:S(2)}) collective-permute-start(bf16[64,1152]{1,0:T(8,128)(2,1)S(1)} %get-tuple-element.53), channel_id=1, source_target_pairs={{0,16},{8,24},{16,0},{24,8},{1,17},{9,25},{17,1},{25,9},{2,18},{10... | collective-permute-start | bytes 442376 | tf_op jit(solution)/shard_map/ppermute | solution.py:458
  28.3 2.5 %collective-permute-start.2 = (bf16[64,1152]{1,0:T(8,128)(2,1)S(1)}, bf16[64,1152]{1,0:T(8,128)(2,1)S(1)}, u32[]{:S(2)}, u32[]{:S(2)}) collective-permute-start(bf16[64,1152]{1,0:T(8,128)(2,1)S(1)} %get-tuple-element.50.refs_0_), channel_id=1, source_target_pairs={{0,8},{8,0},{16,24},{24,16},{1,9},{9,1},{17,25},{25,17},{2,10},{10... | collective-permute-start | bytes 442376 | tf_op jit(solution)/shard_map/ppermute | solution.py:477
  30.8 1.4 %collective-permute-start.4 = (bf16[64,1152]{1,0:T(8,128)(2,1)S(1)}, bf16[64,1152]{1,0:T(8,128)(2,1)S(1)}, u32[]{:S(2)}, u32[]{:S(2)}) collective-permute-start(bf16[64,1152]{1,0:T(8,128)(2,1)S(1)} %get-tuple-element.54.refs_2_.own_ref), channel_id=1, source_target_pairs={{0,8},{8,0},{16,24},{24,16},{1,9},{9,1},{17,25},{25,17},{2,10},{10... | collective-permute-start | bytes 442376 | tf_op jit(solution)/shard_map/ppermute | solution.py:483
  30.8 5.6 %copy-start.1 = (bf16[64,720]{1,0:T(8,128)(2,1)S(1)}, bf16[64,720]{1,0:T(8,128)(2,1)}, u32[]{:S(2)}) copy-start(bf16[64,720]{1,0:T(8,128)(2,1)} %copy-done) | copy-start | bytes 276484
  30.9 5.6 %copy-start.3 = (bf16[64,720]{1,0:T(8,128)(2,1)S(1)}, bf16[64,720]{1,0:T(8,128)(2,1)}, u32[]{:S(2)}) copy-start(bf16[64,720]{1,0:T(8,128)(2,1)} %copy-done.2) | copy-start | bytes 276484
  30.9 5.6 %copy-start.4 = (s32[4,4]{1,0:T(4,128)S(1)}, s32[4,4]{1,0:T(4,128)}, u32[]{:S(2)}) copy-start(s32[4,4]{1,0:T(4,128)} %ids_ref.1) | copy-start | bytes 196
  33.3 10.6 %all-to-all-start.1 = ((bf16[32,4,384]{2,1,0:T(4,128)(2,1)}), bf16[32,4,384]{2,1,0:T(4,128)(2,1)S(1)}, u32[]{:S(2)}, u32[]{:S(2)}) async-start(bf16[32,4,384]{2,1,0:T(4,128)(2,1)} %shard_map.121), calls=%async_computation.1 | async-start | bytes 196608 | tf_op jit(solution)/shard_map/all_to_all | solution.py:519
